TPU v7x, 128 devices: a whole 4x4x4 slice. The times are simulated.
128 devices in a mesh: comp: 16 (over z, y), band: 8 (over x, core).
Axes of the slice: x: 4, y: 4, z: 4, core: 2. Of those that a mesh axis runs over, the one named last changes fastest.
Arguments:
- spectra: bfloat16 [32, 36, 32, 1440], P('comp', None, 'band'), may hold values from 0 to 6, as said below
- depth_class: int32 [32, 1440], P('band'), may hold values from 0 to 63
- group_speed: float32 [64, 32], replicated, may hold values from 0.15 to 0.5
- current: float32 [2, 32, 1440], P(None, 'band'), may hold values from -0.3 to 0.3
- depth_slope: float32 [2, 32, 1440], P(None, 'band'), may hold values from -4 to 4
- wind: float32 [2, 32, 1440], P(None, 'band'), may hold values from -32 to 32
- land_mask: int32 [32, 1440], P('band'), may hold values from 0 to 1, as said below
- block_counts: int32 [8, 16], P('band'), may hold values from 105 to 315, as said below
Outputs:
- spectra_out: bfloat16 [1152, 40320], P(None, ('comp', 'band'))
Inputs may be any that keep to these rules, and one draw needn't show every extreme that they name: `spectra`: nonnegative densities. `land_mask`: band b's rows hold exactly as many sea cells as row b of block_counts sums to. `block_counts`: in every band one block has exactly 315 sea points.
All inputs are finite; a program needn't handle non-finite values.
Results may differ from a plain program's by a relative error of at most 0.0004.
Values may be sent and summed in bfloat16 or wider, within the bound.
A program may use at most 64 MiB of HBM per device.

v0:
```python
import math

import jax
import jax.numpy as jnp
from jax import lax
from jax.sharding import PartitionSpec as P

GROWTH_RATE = 0.05
DAMPING = 1.5
TURNING_SCALE = 0.5


def extended(x, sides, width):
    for axis, dim in sides:
        size, length = (lax.axis_size(axis), x.shape[dim])
        up = [(i, (i + 1) % size) for i in range(size - 1)]
        down = [(j, i) for i, j in up]
        last = lax.slice_in_dim(x, length - width, length, axis=dim)
        initial = lax.slice_in_dim(x, 0, width, axis=dim)
        before = lax.ppermute(last, axis, up)
        after = lax.ppermute(initial, axis, down)
        x = jnp.concatenate([before, x, after], axis=dim)
    return x


def upwind(far_behind, behind, centre, ahead, far_ahead, celerity):
    forward = (2.0 * ahead + 3.0 * centre - 6.0 * behind + far_behind) / 6.0
    backward = (-far_ahead + 6.0 * ahead - 3.0 * centre - 2.0 * behind) / 6.0
    return celerity * jnp.where(celerity > 0, forward, backward)


def wrapped(values, celerity, axis):
    return upwind(
        jnp.roll(values, 2, axis),
        jnp.roll(values, 1, axis),
        values,
        jnp.roll(values, -1, axis),
        jnp.roll(values, -2, axis),
        celerity,
    )


def frequencies(count):
    angular = 2.0 * math.pi * 0.0418 * jnp.power(1.1, jnp.arange(count, dtype=jnp.float32))
    return (angular / angular[-1], 9.81 / angular)


def angles(count):
    heading = jnp.arange(count, dtype=jnp.float32) * (2.0 * math.pi / count)
    return (jnp.cos(heading), jnp.sin(heading))


def block_lists(band_mask, block_sizes, slot_count):
    sea_flag = (band_mask.reshape(-1) == 0).astype(jnp.int32)
    cell_count = sea_flag.shape[0]
    running = jnp.cumsum(sea_flag)
    starts = jnp.cumsum(block_sizes) - block_sizes
    slot_ids = jnp.arange(slot_count, dtype=jnp.int32)
    wanted = starts[:, None] + slot_ids[None, :] + 1
    found = jnp.searchsorted(running, wanted.reshape(-1), side="left")
    found = jnp.minimum(found, cell_count - 1).reshape(wanted.shape)
    return jnp.where(slot_ids[None, :] < block_sizes[:, None], found, -1)


def sources(values, mean_sq, wind_u, wind_v, ratio, phase, cos_t, sin_t):
    strength = jnp.sqrt(mean_sq + 1e-06)
    wind_along = (
        wind_u[None, None, :] * cos_t[None, :, None] + wind_v[None, None, :] * sin_t[None, :, None]
    )
    growth = (
        GROWTH_RATE
        * ratio[:, None, None]
        * jnp.maximum(wind_along / phase[:, None, None] - 1.0, 0.0)
    )
    decay = DAMPING * ratio[:, None, None] * strength[None, None, :]
    return values * jnp.exp(growth - decay)


def body(spectra, depth_class, group_speed, current, depth_slope, wind, land_mask, block_counts):
    freq_dev, dir_count, row_count, lon_count = spectra.shape
    depth_count, total_freqs = group_speed.shape
    groups = lax.axis_size("comp")
    slot_count = row_count * lon_count * 7 // (8 * groups)
    comp_index = lax.axis_index("comp")
    band_index = lax.axis_index("band")
    total_rows = row_count * lax.axis_size("band")
    sea_flag = (land_mask == 0).astype(jnp.float32)
    cos_t, sin_t = angles(dir_count)
    ratio, phase = frequencies(total_freqs)
    selector = (
        depth_class.reshape(1, -1) == jnp.arange(depth_count, dtype=jnp.int32)[:, None]
    ).astype(jnp.float32)
    speeds = jnp.dot(group_speed.T, selector, precision=lax.Precision.HIGHEST).reshape(
        total_freqs, row_count, lon_count
    )
    celerity = lax.dynamic_slice_in_dim(speeds, comp_index * freq_dev, freq_dev, 0)[:, None]
    row_ids = (band_index * row_count + jnp.arange(row_count, dtype=jnp.int32)).astype(jnp.float32)
    latitude = (-60.0 + 120.0 * (row_ids + 0.5) / total_rows) * (math.pi / 180.0)
    stretch = 1.0 / jnp.cos(latitude)
    masked = spectra * sea_flag.astype(jnp.bfloat16)
    padded = extended(masked, (("band", 2),), 2).astype(jnp.float32)
    density = padded[:, :, 2:-2]
    speed_x = celerity * cos_t[None, :, None, None] * stretch[None, None, :, None] + current[0]
    speed_y = celerity * sin_t[None, :, None, None] + current[1]
    across = upwind(
        padded[:, :, :-4],
        padded[:, :, 1:-3],
        density,
        padded[:, :, 3:-1],
        padded[:, :, 4:],
        speed_y,
    )
    advected = (density - wrapped(density, speed_x, 3) - across) * sea_flag
    turning = (
        TURNING_SCALE
        * celerity
        * (
            sin_t[None, :, None, None] * depth_slope[0]
            - cos_t[None, :, None, None] * depth_slope[1]
        )
    )
    refracted = (advected - wrapped(advected, turning, 1)) * sea_flag
    slot_cells = block_lists(land_mask, block_counts[0], slot_count)
    own_cells = lax.dynamic_index_in_dim(slot_cells, comp_index, 0, keepdims=False)
    occupied = (own_cells >= 0).astype(jnp.float32)
    all_cells = jnp.maximum(slot_cells, 0).reshape(-1)
    wind_east = wind[0].reshape(-1)
    wind_north = wind[1].reshape(-1)
    flattened = refracted.reshape(freq_dev * dir_count, row_count * lon_count)
    picked = jnp.take(flattened, all_cells, axis=1).reshape(
        freq_dev * dir_count, groups, slot_count
    )
    arrived = lax.all_to_all(picked, "comp", split_axis=1, concat_axis=0, tiled=True)
    values = arrived.reshape(total_freqs, dir_count, slot_count)
    mean_sq = jnp.mean(values * values, axis=(0, 1))
    safe_cells = jnp.maximum(own_cells, 0)
    finished = sources(
        values,
        mean_sq,
        jnp.take(wind_east, safe_cells),
        jnp.take(wind_north, safe_cells),
        ratio,
        phase,
        cos_t,
        sin_t,
    )
    result = (
        (finished * occupied[None, None, :])
        .astype(jnp.bfloat16)
        .reshape(total_freqs * dir_count, slot_count)
    )
    return result


def solution(mesh):
    return jax.shard_map(
        body,
        mesh=mesh,
        in_specs=(
            P("comp", None, "band", None),
            P("band", None),
            P(),
            P(None, "band", None),
            P(None, "band", None),
            P(None, "band", None),
            P("band", None),
            P("band", None),
        ),
        out_specs=P(None, ("comp", "band")),
        check_vma=False,
    )
```

profile of v0, /device:TPU:1, one launch (start us, length us, event | category | flops | bytes accessed | tf_op | source)
XLA Modules:
  0.0 471.5 jit_solution(16564114170573734932)
XLA Ops:
  3.1 4.5 collective-permute-start
  7.6 1.9 collective-permute-start.1
  10.2 1.6 reshape.272
  12.9 372.6 %while.24 = (s32[]{:T(128)}, u32[5040]{0:T(1024)S(1)}, u32[5040]{0:T(1024)S(1)}, s32[5760]{0:T(1024)S(1)}, s32[16]{0:T(128)S(1)}, /*index=5*/s32[]{:T(128)}, s32[]{:T(128)}, s32[]{}) while((s32[]{:T(128)}, u32[5040]{0:T(1024)S(1)}, u32[5040]{0:T(1024)S(1)}, s32[5760]{0:T(1024)S(1)}, s32[16]{0:T(128)S(1)}, /*index=5*/s32[]{:T(128)}, ...), condition=%wide.region_4.5_spmd.clone, body=%wide.region_3.4_spmd.clone.sunk | while | flops 105924 | bytes 433933 | solution.py:60
  13.2 28.4 %gather_fusion = s32[5040]{0:T(1024)S(1)} fusion(s32[5760]{0:T(1024)S(1)} %get-tuple-element.197, u32[5120]{0:T(1024)S(1)} %pad_clamp_fusion.4), kind=kCustom, calls=%fused_computation.clone.clone.1 | custom fusion | bytes 60480 | tf_op jit(solution)/shard_map/jit(searchsorted)/jit(_searchsorted_scan_impl)/vmap(jit(_searchsorted_scan_impl))/while/body/eval_jaxpr/gather | solution.py:60
  41.8 28.4 %gather_fusion = s32[5040]{0:T(1024)S(1)} fusion(s32[5760]{0:T(1024)S(1)} %get-tuple-element.197, u32[5120]{0:T(1024)S(1)} %pad_clamp_fusion.4), kind=kCustom, calls=%fused_computation.clone.clone.1 | custom fusion | bytes 60480 | tf_op jit(solution)/shard_map/jit(searchsorted)/jit(_searchsorted_scan_impl)/vmap(jit(_searchsorted_scan_impl))/while/body/eval_jaxpr/gather | solution.py:60
  70.5 28.4 %gather_fusion = s32[5040]{0:T(1024)S(1)} fusion(s32[5760]{0:T(1024)S(1)} %get-tuple-element.197, u32[5120]{0:T(1024)S(1)} %pad_clamp_fusion.4), kind=kCustom, calls=%fused_computation.clone.clone.1 | custom fusion | bytes 60480 | tf_op jit(solution)/shard_map/jit(searchsorted)/jit(_searchsorted_scan_impl)/vmap(jit(_searchsorted_scan_impl))/while/body/eval_jaxpr/gather | solution.py:60
  99.1 28.4 %gather_fusion = s32[5040]{0:T(1024)S(1)} fusion(s32[5760]{0:T(1024)S(1)} %get-tuple-element.197, u32[5120]{0:T(1024)S(1)} %pad_clamp_fusion.4), kind=kCustom, calls=%fused_computation.clone.clone.1 | custom fusion | bytes 60480 | tf_op jit(solution)/shard_map/jit(searchsorted)/jit(_searchsorted_scan_impl)/vmap(jit(_searchsorted_scan_impl))/while/body/eval_jaxpr/gather | solution.py:60
  127.8 28.4 %gather_fusion = s32[5040]{0:T(1024)S(1)} fusion(s32[5760]{0:T(1024)S(1)} %get-tuple-element.197, u32[5120]{0:T(1024)S(1)} %pad_clamp_fusion.4), kind=kCustom, calls=%fused_computation.clone.clone.1 | custom fusion | bytes 60480 | tf_op jit(solution)/shard_map/jit(searchsorted)/jit(_searchsorted_scan_impl)/vmap(jit(_searchsorted_scan_impl))/while/body/eval_jaxpr/gather | solution.py:60
  156.4 28.4 %gather_fusion = s32[5040]{0:T(1024)S(1)} fusion(s32[5760]{0:T(1024)S(1)} %get-tuple-element.197, u32[5120]{0:T(1024)S(1)} %pad_clamp_fusion.4), kind=kCustom, calls=%fused_computation.clone.clone.1 | custom fusion | bytes 60480 | tf_op jit(solution)/shard_map/jit(searchsorted)/jit(_searchsorted_scan_impl)/vmap(jit(_searchsorted_scan_impl))/while/body/eval_jaxpr/gather | solution.py:60
  185.0 28.4 %gather_fusion = s32[5040]{0:T(1024)S(1)} fusion(s32[5760]{0:T(1024)S(1)} %get-tuple-element.197, u32[5120]{0:T(1024)S(1)} %pad_clamp_fusion.4), kind=kCustom, calls=%fused_computation.clone.clone.1 | custom fusion | bytes 60480 | tf_op jit(solution)/shard_map/jit(searchsorted)/jit(_searchsorted_scan_impl)/vmap(jit(_searchsorted_scan_impl))/while/body/eval_jaxpr/gather | solution.py:60
  213.7 28.4 %gather_fusion = s32[5040]{0:T(1024)S(1)} fusion(s32[5760]{0:T(1024)S(1)} %get-tuple-element.197, u32[5120]{0:T(1024)S(1)} %pad_clamp_fusion.4), kind=kCustom, calls=%fused_computation.clone.clone.1 | custom fusion | bytes 60480 | tf_op jit(solution)/shard_map/jit(searchsorted)/jit(_searchsorted_scan_impl)/vmap(jit(_searchsorted_scan_impl))/while/body/eval_jaxpr/gather | solution.py:60
  242.3 28.4 %gather_fusion = s32[5040]{0:T(1024)S(1)} fusion(s32[5760]{0:T(1024)S(1)} %get-tuple-element.197, u32[5120]{0:T(1024)S(1)} %pad_clamp_fusion.4), kind=kCustom, calls=%fused_computation.clone.clone.1 | custom fusion | bytes 60480 | tf_op jit(solution)/shard_map/jit(searchsorted)/jit(_searchsorted_scan_impl)/vmap(jit(_searchsorted_scan_impl))/while/body/eval_jaxpr/gather | solution.py:60
  271.0 28.4 %gather_fusion = s32[5040]{0:T(1024)S(1)} fusion(s32[5760]{0:T(1024)S(1)} %get-tuple-element.197, u32[5120]{0:T(1024)S(1)} %pad_clamp_fusion.4), kind=kCustom, calls=%fused_computation.clone.clone.1 | custom fusion | bytes 60480 | tf_op jit(solution)/shard_map/jit(searchsorted)/jit(_searchsorted_scan_impl)/vmap(jit(_searchsorted_scan_impl))/while/body/eval_jaxpr/gather | solution.py:60
  299.6 28.4 %gather_fusion = s32[5040]{0:T(1024)S(1)} fusion(s32[5760]{0:T(1024)S(1)} %get-tuple-element.197, u32[5120]{0:T(1024)S(1)} %pad_clamp_fusion.4), kind=kCustom, calls=%fused_computation.clone.clone.1 | custom fusion | bytes 60480 | tf_op jit(solution)/shard_map/jit(searchsorted)/jit(_searchsorted_scan_impl)/vmap(jit(_searchsorted_scan_impl))/while/body/eval_jaxpr/gather | solution.py:60
  328.3 28.4 %gather_fusion = s32[5040]{0:T(1024)S(1)} fusion(s32[5760]{0:T(1024)S(1)} %get-tuple-element.197, u32[5120]{0:T(1024)S(1)} %pad_clamp_fusion.4), kind=kCustom, calls=%fused_computation.clone.clone.1 | custom fusion | bytes 60480 | tf_op jit(solution)/shard_map/jit(searchsorted)/jit(_searchsorted_scan_impl)/vmap(jit(_searchsorted_scan_impl))/while/body/eval_jaxpr/gather | solution.py:60
  356.9 28.4 %gather_fusion = s32[5040]{0:T(1024)S(1)} fusion(s32[5760]{0:T(1024)S(1)} %get-tuple-element.197, u32[5120]{0:T(1024)S(1)} %pad_clamp_fusion.4), kind=kCustom, calls=%fused_computation.clone.clone.1 | custom fusion | bytes 60480 | tf_op jit(solution)/shard_map/jit(searchsorted)/jit(_searchsorted_scan_impl)/vmap(jit(_searchsorted_scan_impl))/while/body/eval_jaxpr/gather | solution.py:60
  389.0 4.7 %fusion.11 = f32[2,36,4,1440]{3,1,2,0:T(8,128)S(1)} fusion(f32[2,36,8,1440]{3,1,2,0:T(8,128)S(1)} %maximum_convert_fusion, f32[2,36,4,1438]{3,1,2,0:T(8,128)S(1)} %get-tuple-element.116, f32[2,36,4,2]{3,1,2,0:T(8,128)S(1)} %get-tuple-element.128, f32[2,36,4,2]{3,1,2,0:T(8,128)S(1)} %get-tuple-element.127, f32[2,36,4,1438]{3,1,2,0:T(8,128)S(1)} %get-tuple-element.115, ...), kind=kLoop, calls=%fused_computation.23 | loop fusion | flops 18662400 | bytes 16704304 | tf_op jit(solution)/shard_map/mul | solution.py:113
  394.7 2.2 fusion.3
  398.1 2.8 reshape.273
  400.9 2.7 copy.20
  403.6 17.6 %gather_fusion.1 = f32[5040,72]{1,0:T(8,128)} fusion(f32[72,5760]{0,1:T(8,128)S(1)} %copy.20, s32[5120]{0:T(1024)S(1)} %pad_clamp_fusion.1), kind=kCustom, calls=%fused_computation.3 | custom fusion | bytes 2923200 | tf_op jit(solution)/shard_map/jit(_take)/gather | solution.py:130
  421.3 2.1 copy.21
  424.8 1.8 copy.22
  426.6 7.8 %all-to-all-start = ((f32[72,16,315]{2,0,1:T(8,128)}), f32[72,16,315]{2,0,1:T(8,128)S(1)}, u32[]{:S(2)}, u32[]{:S(2)}) async-start(f32[72,16,315]{2,0,1:T(8,128)} %copy.22), calls=%async_computation | async-start | bytes 3538944 | tf_op jit(solution)/shard_map/all_to_all | solution.py:133
  436.0 2.2 gather_fusion.2
  438.2 2.2 gather_fusion.3
  442.0 1.6 div.105
  449.7 11.4 %all-to-all-done = f32[72,16,315]{2,0,1:T(8,128)S(1)} async-done(((f32[72,16,315]{2,0,1:T(8,128)}), f32[72,16,315]{2,0,1:T(8,128)S(1)}, u32[]{:S(2)}, u32[]{:S(2)}) %all-to-all-start) | async-done | bytes 1451552 | tf_op jit(solution)/shard_map/all_to_all | solution.py:133
  463.5 2.6 sub.90
  466.1 3.3 fusion.32
  469.4 2.2 copy.23
  (171 shorter events, 26.1 us)
Async XLA Ops:
  0.0 9.7 %copy-start = (f32[64,32]{0,1:T(8,128)S(1)}, f32[64,32]{0,1:T(8,128)}, u32[]{:S(2)}) copy-start(f32[64,32]{0,1:T(8,128)} %param.14) | copy-start | bytes 24580
  0.8 8.8 %copy-start.4 = (s32[4,1440]{1,0:T(4,128)S(1)}, s32[4,1440]{1,0:T(4,128)}, u32[]{:S(2)}) copy-start(s32[4,1440]{1,0:T(4,128)} %param.13) | copy-start | bytes 69124
  2.2 9.7 %copy-start.1 = (f32[2,4,1440]{2,1,0:T(4,128)S(1)}, f32[2,4,1440]{2,1,0:T(4,128)}, u32[]{:S(2)}) copy-start(f32[2,4,1440]{2,1,0:T(4,128)} %param.15) | copy-start | bytes 138244
  2.2 9.8 %copy-start.2 = (f32[2,4,1440]{2,1,0:T(4,128)S(1)}, f32[2,4,1440]{2,1,0:T(4,128)}, u32[]{:S(2)}) copy-start(f32[2,4,1440]{2,1,0:T(4,128)} %param.16) | copy-start | bytes 138244
  2.2 10.5 %copy-start.5 = (s32[1,16]{1,0:T(1,128)S(1)}, s32[1,16]{1,0:T(1,128)}, u32[]{:S(2)}) copy-start(s32[1,16]{1,0:T(1,128)} %param.19) | copy-start | bytes 196
  3.1 383.9 %collective-permute-start = (bf16[2,36,2,1440]{3,1,2,0:T(8,128)(2,1)}, bf16[2,36,2,1440]{3,1,2,0:T(8,128)(2,1)S(1)}, u32[]{:S(2)}, u32[]{:S(2)}) collective-permute-start(bf16[2,36,2,1440]{3,1,2,0:T(8,128)(2,1)} %get-tuple-element.129), channel_id=1, source_target_pairs={{0,1},{1,2},{2,3},{3,4},{4,5},{5,6},{6,7},{8,9},{9,10},{10,11},{11... | collective-permute-start | bytes 1244168 | tf_op jit(solution)/shard_map/ppermute | solution.py:20
  7.6 379.4 %collective-permute-start.1 = (bf16[2,36,2,1440]{3,1,2,0:T(8,128)(2,1)S(1)}, bf16[2,36,2,1440]{3,1,2,0:T(8,128)(2,1)S(1)}, u32[]{:S(2)}, u32[]{:S(2)}) collective-permute-start(bf16[2,36,2,1440]{3,1,2,0:T(8,128)(2,1)S(1)} %get-tuple-element.130), channel_id=1, source_target_pairs={{1,0},{2,1},{3,2},{4,3},{5,4},{6,5},{7,6},{9,8},{10,9},{11,10},{12... | collective-permute-start | bytes 1244168 | tf_op jit(solution)/shard_map/ppermute | solution.py:21
  12.9 374.0 %copy-start.3 = (f32[2,4,1440]{2,1,0:T(4,128)S(1)}, f32[2,4,1440]{2,1,0:T(4,128)}, u32[]{:S(2)}) copy-start(f32[2,4,1440]{2,1,0:T(4,128)} %param.17) | copy-start | bytes 138244
  426.6 34.5 %all-to-all-start = ((f32[72,16,315]{2,0,1:T(8,128)}), f32[72,16,315]{2,0,1:T(8,128)S(1)}, u32[]{:S(2)}, u32[]{:S(2)}) async-start(f32[72,16,315]{2,0,1:T(8,128)} %copy.22), calls=%async_computation | async-start | bytes 3538944 | tf_op jit(solution)/shard_map/all_to_all | solution.py:133
where the time goes:
time: 472 us
  local copies, waits for them, and re-layouts  424 us (90%)
  other arithmetic  20 us (4%)
  starting transfers between devices  14.2 us (3%)
  waiting for transfers between devices  11.4 us (2%)
    gather x13, local copies, waits for them, and re-layouts, block_lists(): found = jnp.searchsorted(running, wanted.reshape(-1), side='left')  369 us
    gather x3, local copies, waits for them, and re-layouts, body(): jnp.take(flattened, all_cells, axis=1)  21.1 us
    all_to_all x1, waiting for transfers between devices, body(): lax.all_to_all(picked, 'comp', split_axis=1, concat_axis=0, tiled=True)  11.4 us
  transfers between devices with their start and end apart: 3, of which 1 were waited for; matrix products, arithmetic and copies ran while one was open for 83% of the time, Pallas kernels for 0%

commit v1 on v0

v1 whole, which is shorter than its diff:
```python
import math

import jax
import jax.numpy as jnp
import numpy as np
from jax import lax
from jax.experimental import pallas as pl
from jax.experimental.pallas import tpu as pltpu
from jax.sharding import PartitionSpec as P

GROWTH_RATE = 0.05
DAMPING = 1.5
TURNING_SCALE = 0.5

FREQS = 2
LANES = 128
ND = 36
ROWS = 4
NLON = 1440
TILES = 12
GROUPS = ROWS * TILES
BLOCKS = 16
SLOTS = 315
STEPS = 96
COMPS = FREQS * ND
PACK = 184

AT_TILE, AT_GROUP, AT_KEEP, AT_LAST = 0, 128, 256, 384
AT_RANK, AT_LEN, AT_FIRST, AT_COUNT = 512, 640, 768, 896

(F_SEA, F_CX, F_CY, F_CUR0, F_CUR1, F_T0, F_T1) = range(7)

MESH = pl.DeviceIdType.MESH


def angles():
    heading = (np.arange(ND, dtype=np.float32) * np.float32(2.0 * math.pi / ND)).astype(np.float64)
    return (np.cos(heading).astype(np.float32), np.sin(heading).astype(np.float32))


def upwind12(far_behind, behind, centre, ahead, far_ahead, speed):
    forward = speed > 0
    down = jnp.where(forward, ahead, behind)
    up = jnp.where(forward, behind, ahead)
    far = jnp.where(forward, far_behind, far_ahead)
    return jnp.abs(speed) * ((2.0 * down + far) + (3.0 * centre - 6.0 * up))


def stencil_kernel(
    trig_ref, tab_ref, spec_ref, dn_ref, up_ref, fields_ref, depth_ref, gs_ref, stretch_ref, wind_ref, loc_ref,
    sb_ref, wsb_ref,
    x_ref, h_ref, adv_ref, t_ref, stage_ref, fl_ref,
):
    lane = lax.broadcasted_iota(jnp.int32, (8, LANES), 1)
    sub = lax.broadcasted_iota(jnp.int32, (8, LANES), 0)
    row = sub // 2
    tail = NLON - (TILES - 1) * LANES

    for j in range(TILES):
        idx = depth_ref[j]
        cel = jnp.take_along_axis(gs_ref[...], idx, axis=1)
        sixth = cel * (1.0 / 6.0)
        fl_ref[F_SEA, j] = fields_ref[0, j]
        fl_ref[F_CX, j] = sixth * stretch_ref[...]
        fl_ref[F_CY, j] = sixth
        fl_ref[F_CUR0, j] = fields_ref[1, j] * (1.0 / 6.0)
        fl_ref[F_CUR1, j] = fields_ref[2, j] * (1.0 / 6.0)
        fl_ref[F_T0, j] = (TURNING_SCALE * sixth) * fields_ref[3, j]
        fl_ref[F_T1, j] = (TURNING_SCALE * sixth) * fields_ref[4, j]

    def load(d, carry):
        base = pl.multiple_of(8 * d, 8)
        for j in range(TILES):
            width = LANES if j < TILES - 1 else tail
            cols = pl.ds(j * LANES, width)
            for f in range(FREQS):
                v = spec_ref[f, d, :, cols].astype(jnp.float32)
                x_ref[j, pl.ds(base + f, 4, stride=2), pl.ds(0, width)] = v
            h_ref[j, pl.ds(base, 4), pl.ds(0, width)] = dn_ref[d, :, cols].astype(jnp.float32)
            h_ref[j, pl.ds(base + 4, 4), pl.ds(0, width)] = up_ref[d, :, cols].astype(jnp.float32)
        return carry

    lax.fori_loop(0, ND, load, 0)

    def advect(d, carry):
        base = pl.multiple_of(8 * d, 8)
        cos_d = trig_ref[0, d]
        sin_d = trig_ref[1, d]
        x = [x_ref[j, pl.ds(base, 8), :] * fl_ref[F_SEA, j] for j in range(TILES - 1)]
        last = jnp.where(lane < tail, x_ref[TILES - 1, pl.ds(base, 8), :], 0.0) * fl_ref[F_SEA, TILES - 1]
        last = jnp.where(
            lane < tail,
            last,
            jnp.where(lane < tail + 2, pltpu.roll(x[0], tail, 1), pltpu.roll(last, LANES - tail, 1)),
        )
        x.append(last)
        r1 = [pltpu.roll(v, 1, 1) for v in x]
        r2 = [pltpu.roll(v, 2, 1) for v in x]
        l1 = [pltpu.roll(v, LANES - 1, 1) for v in x]
        l2 = [pltpu.roll(v, LANES - 2, 1) for v in x]
        for j in range(TILES):
            before, after = (j - 1) % TILES, (j + 1) % TILES
            v = x[j]
            behind = jnp.where(lane < 1, r1[before], r1[j])
            far_behind = jnp.where(lane < 2, r2[before], r2[j])
            ahead = jnp.where(lane >= LANES - 1, l1[after], l1[j])
            far_ahead = jnp.where(lane >= LANES - 2, l2[after], l2[j])
            speed = fl_ref[F_CX, j] * cos_d + fl_ref[F_CUR0, j]
            along = upwind12(far_behind, behind, v, ahead, far_ahead, speed)
            h = h_ref[j, pl.ds(base, 8), :]
            ahead = pltpu.roll(jnp.where(row == 0, h, v), 6, 0)
            far_ahead = pltpu.roll(jnp.where(row < 2, h, v), 4, 0)
            far_behind = pltpu.roll(jnp.where(row < 2, v, h), 4, 0)
            behind = pltpu.roll(jnp.where(row == 3, h, v), 2, 0)
            speed = fl_ref[F_CY, j] * sin_d + fl_ref[F_CUR1, j]
            across = upwind12(far_behind, behind, v, ahead, far_ahead, speed)
            out = (v - along - across) * fl_ref[F_SEA, j]
            if j == TILES - 1:
                out = jnp.where(lane < tail, out, 0.0)
            adv_ref[j, pl.ds(base, 8), :] = out
        return carry

    lax.fori_loop(0, ND, advect, 0)

    def refract(d, carry):
        cos_d = trig_ref[0, d]
        sin_d = trig_ref[1, d]

        def at(shift):
            k = d + shift
            k = jnp.where(k < 0, k + ND, jnp.where(k >= ND, k - ND, k))
            return pl.multiple_of(8 * k, 8)

        places = [at(s) for s in (-2, -1, 0, 1, 2)]
        for j in range(TILES):
            values = [adv_ref[j, pl.ds(p, 8), :] for p in places]
            speed = fl_ref[F_T0, j] * sin_d - fl_ref[F_T1, j] * cos_d
            out = (values[2] - upwind12(*values, speed)) * fl_ref[F_SEA, j]
            t_ref[j, pl.ds(d, 8, stride=ND), :] = out
        return carry

    lax.fori_loop(0, ND, refract, 0)

    lane_wide = lax.broadcasted_iota(jnp.int32, (COMPS, LANES), 1)

    def step(k, carry):
        acc, wacc = carry
        tile = tab_ref[AT_TILE + k]
        group = tab_ref[AT_GROUP + k]
        keep = tab_ref[AT_KEEP + k].astype(jnp.float32)
        r = group // TILES
        j = group - r * TILES
        local = lane + (tab_ref[AT_RANK + tile] - tab_ref[AT_FIRST + group])
        valid = (lane < tab_ref[AT_LEN + tile]) & (local >= 0) & (local < tab_ref[AT_COUNT + group])
        local = jnp.clip(local, 0, LANES - 1)
        cells = jnp.broadcast_to(loc_ref[pl.ds(group, 1), :], (8, LANES))
        idx = jnp.take_along_axis(cells, local, axis=1)
        parts = []
        for m in range(COMPS // 8):
            data = t_ref[j, pl.ds(pl.multiple_of(r * COMPS, 8) + 8 * m, 8), :]
            got = jnp.take_along_axis(data, idx, axis=1)
            part = jnp.where(valid, got, acc[m] * keep)
            stage_ref[k, pl.ds(8 * m, 8), :] = part
            parts.append(part)
        got = jnp.take_along_axis(wind_ref[group], idx, axis=1)
        wacc = jnp.where(valid, got, wacc * keep)
        stage_ref[k, pl.ds(COMPS, 8), :] = wacc
        return (tuple(parts), wacc)

    zero = jnp.zeros((8, LANES), jnp.float32)
    lax.fori_loop(0, STEPS, step, ((zero,) * (COMPS // 8), zero))

    def gather_out(c, carry):
        for j in range(2):
            k = tab_ref[AT_LAST + 3 * c + j]
            sb_ref[c, pl.ds(COMPS * j, COMPS), :] = stage_ref[k, pl.ds(0, COMPS), :]
            wsb_ref[c, j] = stage_ref[k, pl.ds(COMPS, 8), :]
        k = tab_ref[AT_LAST + 3 * c + 2]
        wsb_ref[c, 2] = stage_ref[k, pl.ds(COMPS, 8), :]
        for m in range(5):
            v = stage_ref[k, pl.ds(8 * m, 8), :]
            if m < 4:
                other = pltpu.roll(stage_ref[k, pl.ds(40 + 8 * m, 8), :], 64, 1)
                v = jnp.where(lane < 64, v, other)
            sb_ref[c, pl.ds(2 * COMPS + 8 * m, 8), :] = v
        return carry

    lax.fori_loop(0, BLOCKS, gather_out, 0)


def exchange_kernel(sb_ref, rb_ref, send_sem, recv_sem, own_sem):
    me = lax.axis_index("comp")
    barrier = pltpu.get_barrier_semaphore()
    for k in range(1, BLOCKS):
        peer = lax.rem(me + k, BLOCKS)
        pl.semaphore_signal(barrier, inc=1, device_id={"comp": peer}, device_id_type=MESH)
    own = pltpu.make_async_copy(sb_ref.at[me], rb_ref.at[me], own_sem)
    own.start()
    pl.semaphore_wait(barrier, BLOCKS - 1)
    copies = []
    for k in range(1, BLOCKS):
        peer = lax.rem(me + k, BLOCKS)
        copy = pltpu.make_async_remote_copy(
            src_ref=sb_ref.at[peer],
            dst_ref=rb_ref.at[me],
            send_sem=send_sem.at[k],
            recv_sem=recv_sem.at[k],
            device_id={"comp": peer},
            device_id_type=MESH,
        )
        copy.start()
        copies.append(copy)
    own.wait()
    for copy in copies:
        copy.wait()


def source_kernel(wind_ref, trig_ref, coef_ref, rb_ref, out_ref, wa_ref, v_ref):
    zero = jnp.zeros((8, LANES), jnp.float32)

    def squares(i, acc):
        acc = list(acc)
        for j in range(3):
            rows = COMPS if j < 2 else 40
            for m in range(rows // 8):
                v = rb_ref[i, pl.ds(COMPS * j + 8 * m, 8), :]
                acc[j] = acc[j] + v * v
        return tuple(acc)

    sums = lax.fori_loop(0, BLOCKS, squares, (zero, zero, zero))
    means = [jnp.sum(s, axis=0, keepdims=True) for s in sums]
    lane1 = lax.broadcasted_iota(jnp.int32, (1, LANES), 1)
    means[2] = jnp.where(lane1 < 64, means[2] + pltpu.roll(means[2], 64, 1), 0.0)
    total = BLOCKS * COMPS
    lane = lax.broadcasted_iota(jnp.int32, (8, LANES), 1)
    sub = lax.broadcasted_iota(jnp.int32, (8, LANES), 0)
    strength = [
        jnp.broadcast_to(jnp.sqrt(m * (1.0 / total) + 1e-6), (8, LANES)) for m in means
    ]
    for j in range(3):
        east = jnp.broadcast_to(wind_ref[j, 0:1, :], (8, LANES))
        north = jnp.broadcast_to(wind_ref[j, 1:2, :], (8, LANES))
        for m in range(COMPS // 8):
            wa_ref[j, pl.ds(8 * m, 8), :] = (
                east * trig_ref[0, pl.ds(8 * m, 8), :] + north * trig_ref[1, pl.ds(8 * m, 8), :]
            )

    def apply(i, carry):
        for j in range(3):
            for m in range(COMPS // 8):
                f0 = (8 * m) // ND
                f1 = (8 * m + 7) // ND

                def coef(q):
                    low = coef_ref[q, 2 * i + f0]
                    if f0 == f1:
                        return low
                    return jnp.where(sub < ND - 8 * m, low, coef_ref[q, 2 * i + f1])

                if j < 2:
                    v = rb_ref[i, pl.ds(COMPS * j + 8 * m, 8), :]
                elif m < 5:
                    v = rb_ref[i, pl.ds(2 * COMPS + 8 * m, 8), :]
                else:
                    v = pltpu.roll(rb_ref[i, pl.ds(2 * COMPS + 8 * (m - 5), 8), :], 64, 1)
                growth = jnp.maximum(wa_ref[j, pl.ds(8 * m, 8), :] * coef(0) - coef(1), 0.0)
                out = v * jnp.exp(growth - strength[j] * coef(2))
                v_ref[j, pl.ds(pl.multiple_of(COMPS * i, 8) + 8 * m, 8), :] = out
        return carry

    lax.fori_loop(0, BLOCKS, apply, 0)

    for m in range(BLOCKS * COMPS // LANES):
        for j in range(3):
            block = v_ref[j, pl.ds(LANES * m, LANES), :].T.astype(jnp.bfloat16)
            rows = min(LANES, SLOTS - LANES * j)
            out_ref[pl.ds(LANES * j, rows), pl.ds(LANES * m, LANES)] = block[:rows]


def tables(land_mask, counts):
    sea = (land_mask == 0).astype(jnp.float32)
    padded = jnp.pad(sea, ((0, 0), (0, TILES * LANES - NLON))).reshape(GROUPS, LANES)
    lanes = np.arange(LANES)
    upper = (lanes[:, None] <= lanes[None, :]).astype(np.float32)
    inclusive = jnp.dot(padded, upper, preferred_element_type=jnp.float32).astype(jnp.int32)
    local = jnp.sum((inclusive[:, :, None] <= lanes[None, None, :].astype(np.int32)).astype(jnp.int32), axis=1)
    local = jnp.minimum(local, LANES - 1)
    count = inclusive[:, LANES - 1]
    groups = np.arange(GROUPS)
    ends = jnp.sum(jnp.where(groups[None, :] <= groups[:, None], count[None, :], 0), axis=1)
    first = ends - count
    blocks = np.arange(BLOCKS)
    starts = jnp.sum(jnp.where(blocks[None, :] < blocks[:, None], counts[None, :], 0), axis=1)
    offset = (np.arange(3) * LANES).astype(np.int32)
    rank = (starts[:, None] + offset[None, :]).reshape(-1)
    length = jnp.clip(counts[:, None] - offset[None, :], 0, LANES).reshape(-1)
    last_rank = rank + jnp.maximum(length, 1) - 1
    low = jnp.minimum(jnp.sum((ends[None, :] <= rank[:, None]).astype(jnp.int32), axis=1), GROUPS - 1)
    high = jnp.minimum(jnp.sum((ends[None, :] <= last_rank[:, None]).astype(jnp.int32), axis=1), GROUPS - 1)
    width = jnp.where(length > 0, high - low + 1, 1)
    tiles = np.arange(3 * BLOCKS)
    stop = jnp.sum(jnp.where(tiles[None, :] <= tiles[:, None], width[None, :], 0), axis=1)
    steps = np.arange(LANES).astype(np.int32)
    tile = jnp.sum((stop[None, :] <= steps[:, None]).astype(jnp.int32), axis=1)
    tile = jnp.minimum(tile, 3 * BLOCKS - 1)
    hit = tile[:, None] == tiles[None, :].astype(np.int32)
    group = steps + jnp.sum(jnp.where(hit, (low - (stop - width))[None, :], 0), axis=1)
    group = jnp.clip(group, 0, GROUPS - 1)
    begin = jnp.sum(jnp.where(hit, (stop - width)[None, :], 0), axis=1)
    keep = (steps > begin).astype(jnp.int32)

    def wide(x):
        return jnp.pad(x.astype(jnp.int32), (0, LANES - x.shape[0]))

    table = jnp.concatenate(
        [tile, group, keep, wide(stop - 1), wide(rank), wide(length), wide(first), wide(count)]
    )
    return table, local


def per_cell(x):
    lead = x.shape[:-2]
    x = jnp.pad(x, ((0, 0),) * (x.ndim - 1) + ((0, TILES * LANES - NLON),))
    x = x.reshape(lead + (ROWS, 1, TILES, LANES))
    x = jnp.broadcast_to(x, lead + (ROWS, FREQS, TILES, LANES))
    x = jnp.moveaxis(x, -2, len(lead))
    return x.reshape(lead + (TILES, 2 * ROWS, LANES))


def body(spectra, depth_class, group_speed, current, depth_slope, wind, land_mask, block_counts):
    comp_index = lax.axis_index("comp")
    band_index = lax.axis_index("band")
    bands = lax.axis_size("band")
    cos_t, sin_t = angles()

    sea = (land_mask == 0).astype(jnp.bfloat16)

    def edge(lo):
        part = spectra[:, :, lo : lo + 2] * sea[lo : lo + 2]
        return jnp.transpose(part, (1, 2, 0, 3)).reshape(ND, 2 * FREQS, NLON)

    up_pairs = [(i, i + 1) for i in range(bands - 1)]
    down_pairs = [(i + 1, i) for i in range(bands - 1)]
    halo_up = lax.ppermute(edge(2), "band", up_pairs)
    halo_dn = lax.ppermute(edge(0), "band", down_pairs)

    table, local = tables(land_mask, block_counts[0])
    fields = per_cell(
        jnp.concatenate([(land_mask == 0).astype(jnp.float32)[None], current, depth_slope], axis=0)
    )
    depth = per_cell(depth_class)
    own = lax.dynamic_slice_in_dim(group_speed, comp_index * FREQS, FREQS, 1)
    own = jnp.pad(own.T, ((0, 0), (0, LANES - own.shape[0])))
    speeds = jnp.tile(own, (ROWS, 1))
    row_ids = (band_index * ROWS + jnp.arange(ROWS, dtype=jnp.int32)).astype(jnp.float32)
    latitude = (-60.0 + 120.0 * (row_ids + 0.5) / (ROWS * bands)) * (math.pi / 180.0)
    stretch = jnp.broadcast_to(jnp.repeat(1.0 / jnp.cos(latitude), FREQS)[:, None], (8, LANES))
    wide_wind = jnp.pad(wind, ((0, 0), (0, 0), (0, TILES * LANES - NLON))).reshape(2, GROUPS, LANES)
    wide_wind = jnp.pad(jnp.moveaxis(wide_wind, 0, 1), ((0, 0), (0, 6), (0, 0)))

    vmem = pl.BlockSpec(memory_space=pltpu.VMEM)
    smem = pl.BlockSpec(memory_space=pltpu.SMEM)
    sb, wsb = pl.pallas_call(
        stencil_kernel,
        out_shape=(
            jax.ShapeDtypeStruct((BLOCKS, PACK, LANES), jnp.float32),
            jax.ShapeDtypeStruct((BLOCKS, 3, 8, LANES), jnp.float32),
        ),
        in_specs=[smem, smem] + [vmem] * 9,
        out_specs=(vmem, vmem),
        scratch_shapes=[
            pltpu.VMEM((TILES, 8 * ND, LANES), jnp.float32),
            pltpu.VMEM((TILES, 8 * ND, LANES), jnp.float32),
            pltpu.VMEM((TILES, 8 * ND, LANES), jnp.float32),
            pltpu.VMEM((TILES, 8 * ND, LANES), jnp.float32),
            pltpu.VMEM((STEPS, COMPS + 8, LANES), jnp.float32),
            pltpu.VMEM((7, TILES, 8, LANES), jnp.float32),
        ],
        compiler_params=pltpu.CompilerParams(vmem_limit_bytes=48 * 1024 * 1024),
        name="stencil",
    )(
        jnp.asarray(np.stack([cos_t, sin_t])),
        table,
        spectra,
        halo_dn,
        halo_up,
        fields,
        depth,
        speeds,
        stretch,
        wide_wind,
        local,
    )

    rb = pl.pallas_call(
        exchange_kernel,
        out_shape=jax.ShapeDtypeStruct((BLOCKS, PACK, LANES), jnp.float32),
        in_specs=[vmem],
        out_specs=vmem,
        scratch_shapes=[
            pltpu.SemaphoreType.DMA((BLOCKS,)),
            pltpu.SemaphoreType.DMA((BLOCKS,)),
            pltpu.SemaphoreType.DMA,
        ],
        compiler_params=pltpu.CompilerParams(
            collective_id=0, has_side_effects=True, vmem_limit_bytes=16 * 1024 * 1024
        ),
        name="exchange",
    )(sb)

    angular = 2.0 * math.pi * 0.0418 * np.power(1.1, np.arange(BLOCKS * FREQS, dtype=np.float64))
    ratio = angular / angular[-1]
    phase = 9.81 / angular
    coef = np.stack([GROWTH_RATE * ratio / phase, GROWTH_RATE * ratio, DAMPING * ratio]).astype(np.float32)
    trig = np.stack([np.tile(cos_t, 2), np.tile(sin_t, 2)])
    trig = np.ascontiguousarray(np.broadcast_to(trig[:, :, None], (2, COMPS, LANES)))
    own_wind = lax.dynamic_index_in_dim(wsb, comp_index, 0, keepdims=False)
    out = pl.pallas_call(
        source_kernel,
        out_shape=jax.ShapeDtypeStruct((SLOTS, BLOCKS * COMPS), jnp.bfloat16),
        in_specs=[vmem, vmem, smem, vmem],
        out_specs=vmem,
        scratch_shapes=[
            pltpu.VMEM((3, COMPS, LANES), jnp.float32),
            pltpu.VMEM((3, BLOCKS * COMPS, LANES), jnp.float32),
        ],
        compiler_params=pltpu.CompilerParams(vmem_limit_bytes=16 * 1024 * 1024),
        name="sources",
    )(own_wind, jnp.asarray(trig), jnp.asarray(coef), rb)
    return out.T


def solution(mesh):
    return jax.shard_map(
        body,
        mesh=mesh,
        in_specs=(
            P("comp", None, "band", None),
            P("band", None),
            P(),
            P(None, "band", None),
            P(None, "band", None),
            P(None, "band", None),
            P("band", None),
            P("band", None),
        ),
        out_specs=P(None, ("comp", "band")),
        check_vma=False,
    )
```

time: 472 us -> 71.6 us (0.15)
  local copies, waits for them, and re-layouts: 424 us -> 2.25 us
  Pallas kernels: 0 us -> 53.7 us
  other arithmetic: 20 us -> 5.38 us
  waiting for transfers between devices: 11.4 us -> 1.98 us
  starting transfers between devices: 14.2 us -> 6.43 us
    gather x18 -> x0, local copies, waits for them, and re-layouts: 394 us -> none  [the longest x13 369 us: block_lists(): found = jnp.searchsorted(running, wanted.reshape(-1), side='left')]
    pallas_call x0 -> x3, Pallas kernels: none -> 53.7 us  [the longest x1 25.3 us: body(): pl.pallas_call(stencil_kernel, out_shape=(jax.ShapeDtypeStruct((BLOCKS, P...]
    mul x8 -> x0, other arithmetic: 11.8 us -> none  [the longest x1 4.75 us: body(): advected = (density - wrapped(density, speed_x, 3) - across) * sea_flag]
    all_to_all x1 -> x0, waiting for transfers between devices: 11.4 us -> none  [body(): lax.all_to_all(picked, 'comp', split_axis=1, concat_axis=0, tiled=True)]
    all_to_all x1 -> x0, starting transfers between devices: 7.78 us -> none  [body(): lax.all_to_all(picked, 'comp', split_axis=1, concat_axis=0, tiled=True)]
    reshape x4 -> x5, local copies, waits for them, and re-layouts: 7.24 us -> 0.67 us  [the longest x2 0.61 us: edge(): return jnp.transpose(part, (1, 2, 0, 3)).reshape(ND, 2 * FREQS, NLON)]
    div x4 -> x0, local copies, waits for them, and re-layouts: 5.12 us -> none  [sources(): wind_along / phase[:, None, None] - 1.0]
    convert_element_type x5 -> x1, other arithmetic: 5.05 us -> 0.01 us  [body(): sea = (land_mask == 0).astype(jnp.bfloat16)]
  transfers between devices with their start and end apart: 3 -> 2, of which waited for: 1 -> 2; matrix products, arithmetic and copies ran while one was open for 83% -> 5% of each run, Pallas kernels for 0% -> 0%
where the time goes in v1:
time: 71.6 us; the launch traced here: 70.3 us
  Pallas kernels  53.7 us (75%)
  starting transfers between devices  6.43 us (9%)
  other arithmetic  5.38 us (8%)
  local copies, waits for them, and re-layouts  2.25 us (3%)
  waiting for transfers between devices  1.98 us (3%)
    pallas_call x1, Pallas kernels, body(): pl.pallas_call(stencil_kernel, out_shape=(jax.ShapeDtypeStruct((BLOCKS, P...  25.3 us
    pallas_call x1, Pallas kernels, body(): pl.pallas_call(exchange_kernel, out_shape=jax.ShapeDtypeStruct((BLOCKS, P...  25.1 us
    ppermute x1, starting transfers between devices, body(): halo_dn = lax.ppermute(edge(0), 'band', down_pairs)  3.33 us
    pallas_call x1, Pallas kernels, body(): pl.pallas_call(source_kernel, out_shape=jax.ShapeDtypeStruct((SLOTS, BLOC...  3.23 us
    ppermute x1, starting transfers between devices, body(): halo_up = lax.ppermute(edge(2), 'band', up_pairs)  3.1 us
    transpose x1, other arithmetic, edge(): return jnp.transpose(part, (1, 2, 0, 3)).reshape(ND, 2 * FREQS, NLON)  2.47 us
    ppermute x1, waiting for transfers between devices, body(): halo_up = lax.ppermute(edge(2), 'band', up_pairs)  1.86 us
  transfers between devices with their start and end apart: 2, of which 2 were waited for; matrix products, arithmetic and copies ran while one was open for 5% of the time, Pallas kernels for 0%

profile of v1, /device:TPU:1, one launch (start us, length us, event | category | flops | bytes accessed | tf_op | source)
XLA Modules:
  0.0 70.3 jit_solution(4303306357237074177)
XLA Ops:
  0.0 0.8 %convert_bitcast_fusion = (f32[1,4,1440]{2,1,0:T(4,128)S(1)}, pred[4,1440]{1,0:T(4,128)(4,1)S(1)}) fusion(s32[4,1440]{1,0:T(4,128)} %param.27), kind=kLoop, calls=%fused_computation.26 | loop fusion | flops 11520 | bytes 51840 | tf_op jit(solution)/shard_map/broadcast_in_dim | solution.py:349
  0.8 2.5 %multiply_bitcast_fusion = (bf16[36,2,2,1440]{3,1,0,2:T(2,128)(2,1)S(1)}, bf16[36,2,2,1440]{3,1,0,2:T(2,128)(2,1)S(1)}) fusion(bf16[2,36,4,1440]{3,2,1,0:T(4,128)(2,1)} %spec_ref.1, bf16[2,1440]{1,0:T(2,128)(2,1)S(1)} %get-tuple-element.19, bf16[2,1440]{1,0:T(2,128)(2,1)S(1)} %get-tuple-element.20), kind=kLoop, calls=%fused_computation.3 | loop fusion | flops 414720 | bytes 1670400 | tf_op jit(solution)/shard_map/transpose | solution.py:340
  3.3 0.3 copy.31
  3.6 0.0 copy-start.11
  3.7 0.0 copy-start.10
  3.7 0.3 reshape.128
  4.0 3.3 %collective-permute-start = (bf16[36,4,1440]{2,1,0:T(4,128)(2,1)S(1)}, bf16[36,4,1440]{2,1,0:T(4,128)(2,1)S(1)}, u32[]{:S(2)}, u32[]{:S(2)}) collective-permute-start(bf16[36,4,1440]{2,1,0:T(4,128)(2,1)S(1)} %reshape.128), channel_id=1, source_target_pairs={{1,0},{2,1},{3,2},{4,3},{5,4},{6,5},{7,6},{9,8},{10,9},{11,10},{12... | collective-permute-start | bytes 1244168 | tf_op jit(solution)/shard_map/ppermute | solution.py:345
  7.4 0.3 copy.32
  7.7 0.0 copy-start.4
  7.7 0.3 reshape.129
  8.1 3.1 %collective-permute-start.1 = (bf16[36,4,1440]{2,1,0:T(4,128)(2,1)S(1)}, bf16[36,4,1440]{2,1,0:T(4,128)(2,1)S(1)}, u32[]{:S(2)}, u32[]{:S(2)}) collective-permute-start(bf16[36,4,1440]{2,1,0:T(4,128)(2,1)S(1)} %reshape.129), channel_id=1, source_target_pairs={{0,1},{1,2},{2,3},{3,4},{4,5},{5,6},{6,7},{8,9},{9,10},{10,11},{11... | collective-permute-start | bytes 1244168 | tf_op jit(solution)/shard_map/ppermute | solution.py:344
  11.2 0.1 select_reduce_fusion.2
  11.3 0.1 broadcast_add_fusion
  11.4 0.1 add.100
  11.5 0.1 min.60
  11.6 0.1 convolution_convert_fusion
  11.8 0.2 slice_reduce_fusion
  12.0 0.1 select_reduce_fusion.1
  12.1 0.2 convert_reduce_fusion.2
  12.3 0.1 select_reduce_fusion
  12.4 0.1 convert_reduce_fusion.1
  12.6 0.1 fusion.4
  12.9 0.1 broadcast_in_dim.105
  13.0 0.1 broadcast_in_dim.106
  13.2 1.2 %convert_reduce_fusion = s32[48,128]{1,0:T(8,128)S(1)} fusion(s32[48,128]{1,0:T(8,128)S(1)} %convolution_convert_fusion), kind=kLoop, calls=%fused_computation.1 | loop fusion | flops 2353152 | bytes 49152 | tf_op jit(solution)/shard_map/reduce_sum | solution.py:286
  14.4 0.1 collective-permute-done.dn_ref
  14.5 1.9 %collective-permute-done.1.up_ref = bf16[36,4,1440]{2,1,0:T(4,128)(2,1)S(1)} collective-permute-done((bf16[36,4,1440]{2,1,0:T(4,128)(2,1)S(1)}, bf16[36,4,1440]{2,1,0:T(4,128)(2,1)S(1)}, u32[]{:S(2)}, u32[]{:S(2)}) %collective-permute-start.1) | collective-permute-done | bytes 414752 | tf_op jit(solution)/shard_map/ppermute | solution.py:344
  16.4 0.1 broadcast_in_dim.107.stretch_ref
  16.5 0.1 broadcast_in_dim.102
  16.6 25.3 %stencil.1 = (f32[16,184,128]{2,1,0:T(8,128)S(1)}, f32[16,3,8,128]{3,2,1,0:T(8,128)S(1)}) custom-call(f32[2,36]{1,0:T(2,128)S(1)} %copy-done.4, s32[1024]{0:T(1024)S(1)} %constant_dynamic-update-slice_fusion.tab_ref, bf16[2,36,4,1440]{3,2,1,0:T(4,128)(2,1)S(1)} %copy-done.1, bf16[36,4,1440]{2,1,0:T(4,128)(2,1)S(1)} %collective-permute-done.dn_ref, ...), custom_call_target="tpu_custom_call" | custom-call | tf_op jit(solution)/shard_map/stencil/pallas_call | solution.py:363
  41.9 25.1 %exchange.1.rb_ref = f32[16,184,128]{2,1,0:T(8,128)S(1)} custom-call(f32[16,184,128]{2,1,0:T(8,128)S(1)} %get-tuple-element.8.sb_ref), custom_call_target="tpu_custom_call" | custom-call | tf_op jit(solution)/shard_map/exchange/pallas_call | solution.py:395
  67.1 3.2 %sources.1 = bf16[315,1152]{1,0:T(8,128)(2,1)} custom-call(f32[3,8,128]{2,1,0:T(8,128)S(1)} %dynamic-slice_bitcast_fusion.wind_ref, f32[2,72,128]{2,1,0:T(8,128)S(1)} %copy-done.2, f32[3,32]{1,0:T(4,128)S(1)} %copy-done.3, f32[16,184,128]{2,1,0:T(8,128)S(1)} %exchange.1.rb_ref), custom_call_target="tpu_custom_call" | custom-call | tf_op jit(solution)/shard_map/sources/pallas_call | solution.py:418
  (54 shorter events, 0.4 us)
Async XLA Ops:
  0.0 12.8 %copy-start = (f32[64,32]{0,1:T(8,128)S(1)}, f32[64,32]{0,1:T(8,128)}, u32[]{:S(2)}) copy-start(f32[64,32]{0,1:T(8,128)} %param.23) | copy-start | bytes 24580
  3.6 7.6 %copy-start.11 = (pred[16,16]{1,0:T(8,128)(4,1)S(1)}, pred[16,16]{1,0:T(8,128)(4,1)}, u32[]{:S(2)}) copy-start(pred[16,16]{1,0:T(8,128)(4,1)} %constant.78.clone) | copy-start | bytes 772
  3.6 7.6 %copy-start.12 = (s32[1,16]{1,0:T(1,128)S(1)}, s32[1,16]{1,0:T(1,128)}, u32[]{:S(2)}) copy-start(s32[1,16]{1,0:T(1,128)} %param.28) | copy-start | bytes 196
  3.7 8.0 %copy-start.8 = (bf16[128,128]{1,0:T(8,128)(2,1)S(1)}, bf16[128,128]{1,0:T(8,128)(2,1)}, u32[]{:S(2)}) copy-start(bf16[128,128]{1,0:T(8,128)(2,1)} %constant.155) | copy-start | bytes 98308
  3.7 8.3 %copy-start.10 = (pred[48,48]{1,0:T(8,128)(4,1)S(1)}, pred[48,48]{1,0:T(8,128)(4,1)}, u32[]{:S(2)}) copy-start(pred[48,48]{1,0:T(8,128)(4,1)} %constant.77.clone) | copy-start | bytes 6916
  3.7 8.9 %copy-start.9 = (s32[4,1440]{1,0:T(4,128)S(1)}, s32[4,1440]{1,0:T(4,128)}, u32[]{:S(2)}) copy-start(s32[4,1440]{1,0:T(4,128)} %param.22) | copy-start | bytes 69124
  3.7 9.1 %copy-start.6 = (f32[2,4,1440]{2,1,0:T(4,128)S(1)}, f32[2,4,1440]{2,1,0:T(4,128)}, u32[]{:S(2)}) copy-start(f32[2,4,1440]{2,1,0:T(4,128)} %param.25) | copy-start | bytes 138244
  3.7 9.1 %copy-start.7 = (f32[2,4,1440]{2,1,0:T(4,128)S(1)}, f32[2,4,1440]{2,1,0:T(4,128)}, u32[]{:S(2)}) copy-start(f32[2,4,1440]{2,1,0:T(4,128)} %param.24) | copy-start | bytes 138244
  3.7 9.3 %copy-start.5 = (f32[2,4,1440]{2,1,0:T(4,128)S(1)}, f32[2,4,1440]{2,1,0:T(4,128)}, u32[]{:S(2)}) copy-start(f32[2,4,1440]{2,1,0:T(4,128)} %param.26) | copy-start | bytes 138244
  4.0 10.5 %collective-permute-start = (bf16[36,4,1440]{2,1,0:T(4,128)(2,1)S(1)}, bf16[36,4,1440]{2,1,0:T(4,128)(2,1)S(1)}, u32[]{:S(2)}, u32[]{:S(2)}) collective-permute-start(bf16[36,4,1440]{2,1,0:T(4,128)(2,1)S(1)} %reshape.128), channel_id=1, source_target_pairs={{1,0},{2,1},{3,2},{4,3},{5,4},{6,5},{7,6},{9,8},{10,9},{11,10},{12... | collective-permute-start | bytes 1244168 | tf_op jit(solution)/shard_map/ppermute | solution.py:345
  7.7 8.9 %copy-start.1 = (bf16[2,36,4,1440]{3,2,1,0:T(4,128)(2,1)S(1)}, bf16[2,36,4,1440]{3,2,1,0:T(4,128)(2,1)}, u32[]{:S(2)}) copy-start(bf16[2,36,4,1440]{3,2,1,0:T(4,128)(2,1)} %spec_ref.1) | copy-start | bytes 2488324
  7.7 8.9 %copy-start.4 = (f32[2,36]{1,0:T(2,128)S(1)}, f32[2,36]{1,0:T(2,128)}, u32[]{:S(2)}) copy-start(f32[2,36]{1,0:T(2,128)} %constant.82.clone.trig_ref) | copy-start | bytes 868
  8.1 8.3 %collective-permute-start.1 = (bf16[36,4,1440]{2,1,0:T(4,128)(2,1)S(1)}, bf16[36,4,1440]{2,1,0:T(4,128)(2,1)S(1)}, u32[]{:S(2)}, u32[]{:S(2)}) collective-permute-start(bf16[36,4,1440]{2,1,0:T(4,128)(2,1)S(1)} %reshape.129), channel_id=1, source_target_pairs={{0,1},{1,2},{2,3},{3,4},{4,5},{5,6},{6,7},{8,9},{9,10},{10,11},{11... | collective-permute-start | bytes 1244168 | tf_op jit(solution)/shard_map/ppermute | solution.py:344
  41.9 25.1 %copy-start.2 = (f32[2,72,128]{2,1,0:T(8,128)S(1)}, f32[2,72,128]{2,1,0:T(8,128)}, u32[]{:S(2)}) copy-start(f32[2,72,128]{2,1,0:T(8,128)} %constant.83.clone.trig_ref) | copy-start | bytes 221188
  41.9 25.2 %copy-start.3 = (f32[3,32]{1,0:T(4,128)S(1)}, f32[3,32]{1,0:T(4,128)}, u32[]{:S(2)}) copy-start(f32[3,32]{1,0:T(4,128)} %constant.84.clone.coef_ref) | copy-start | bytes 1156

commit v2 on v1

v2 whole, which is shorter than its diff:
```python
import math

import jax
import jax.numpy as jnp
import numpy as np
from jax import lax
from jax.experimental import pallas as pl
from jax.experimental.pallas import tpu as pltpu
from jax.sharding import PartitionSpec as P

GROWTH_RATE = 0.05
DAMPING = 1.5
TURNING_SCALE = 0.5

FREQS = 2
LANES = 128
ND = 36
ROWS = 4
NLON = 1440
TILES = 12
GROUPS = ROWS * TILES
BLOCKS = 16
SLOTS = 315
STEPS = 96
COMPS = FREQS * ND
PACK = 192
CHUNKS = 4
PER = TILES // CHUNKS
SIDE = 4

AT_TILE, AT_GROUP, AT_KEEP, AT_LAST = 0, 128, 256, 384
AT_RANK, AT_LEN, AT_FIRST, AT_COUNT = 512, 640, 768, 896
AT_SPOT = 1024

(F_SEA, F_CX, F_CY, F_CUR0, F_CUR1, F_T0, F_T1, F_W0, F_W1) = range(9)

MESH = pl.DeviceIdType.MESH


def angles():
    heading = (np.arange(ND, dtype=np.float32) * np.float32(2.0 * math.pi / ND)).astype(np.float64)
    return (np.cos(heading).astype(np.float32), np.sin(heading).astype(np.float32))


def upwind12(far_behind, behind, centre, ahead, far_ahead, speed):
    forward = speed > 0
    down = jnp.where(forward, ahead, behind)
    up = jnp.where(forward, behind, ahead)
    far = jnp.where(forward, far_behind, far_ahead)
    return jnp.abs(speed) * ((2.0 * down + far) + (3.0 * centre - 6.0 * up))


OFFSETS = sorted(
    [(a, b) for a in range(SIDE) for b in range(SIDE) if a or b],
    key=lambda o: -(min(o[0], SIDE - o[0]) + min(o[1], SIDE - o[1])),
)


def step_kernel(
    trig_ref, tab_ref, coef_ref, spec_ref, fields_ref, depth_ref, gs_ref, stretch_ref, loc_ref,
    rb_ref,
    x_ref, adv_ref, t_ref, stage_ref, idx_ref, dec_ref, fl_ref, hs_ref, hr_ref, sq_ref, part_ref, total_ref, level_ref, yr_ref, zr_ref, sb_ref,
    halo_send, halo_recv, sum_send, sum_recv, send_sem, recv_sem,
):
    lane = lax.broadcasted_iota(jnp.int32, (8, LANES), 1)
    sub = lax.broadcasted_iota(jnp.int32, (8, LANES), 0)
    row = sub // 2
    tail = NLON - (TILES - 1) * LANES
    me = lax.axis_index("comp")
    band = lax.axis_index("band")
    bands = lax.axis_size("band")
    z, y = me // SIDE, lax.rem(me, SIDE)
    north = lax.rem(band + 1, bands)
    south = lax.rem(band + bands - 1, bands)

    def peer(o):
        return lax.rem(z + o[0], SIDE) * SIDE + lax.rem(y + o[1], SIDE)

    barrier = pltpu.get_barrier_semaphore()
    for b in (north, south):
        pl.semaphore_signal(barrier, inc=1, device_id={"band": b}, device_id_type=MESH)
    for o in OFFSETS:
        pl.semaphore_signal(barrier, inc=1, device_id={"comp": peer(o)}, device_id_type=MESH)

    for j in range(TILES):
        cel = jnp.take_along_axis(gs_ref[...], depth_ref[j], axis=1)
        sixth = cel * (1.0 / 6.0)
        fl_ref[F_SEA, j] = fields_ref[0, j]
        fl_ref[F_CX, j] = sixth * stretch_ref[...]
        fl_ref[F_CY, j] = sixth
        fl_ref[F_CUR0, j] = fields_ref[1, j] * (1.0 / 6.0)
        fl_ref[F_CUR1, j] = fields_ref[2, j] * (1.0 / 6.0)
        fl_ref[F_T0, j] = (TURNING_SCALE * sixth) * fields_ref[3, j]
        fl_ref[F_T1, j] = (TURNING_SCALE * sixth) * fields_ref[4, j]

    even = lax.rem(sub, 2) == 0
    grow_a = jnp.where(even, coef_ref[0, FREQS * me], coef_ref[0, FREQS * me + 1])
    grow_b = jnp.where(even, coef_ref[1, FREQS * me], coef_ref[1, FREQS * me + 1])

    for j in range(TILES):
        fl_ref[F_W0, j] = fields_ref[5, j] * grow_a
        fl_ref[F_W1, j] = fields_ref[6, j] * grow_a

    def load(d, carry):
        base = pl.multiple_of(8 * d, 8)
        for j in range(TILES):
            width = LANES if j < TILES - 1 else tail
            for f in range(FREQS):
                v = spec_ref[f, d, :, pl.ds(j * LANES, width)].astype(jnp.float32)
                x_ref[j, pl.ds(base + f, 4, stride=2), pl.ds(0, width)] = v
        return carry

    lax.fori_loop(0, ND, load, 0)

    def prepare(q, carry):
        base = pl.multiple_of(32 * q, 32)
        first = [None] * 4
        for j in range(TILES):
            v = [x_ref[j, pl.ds(base + 8 * i, 8), :] for i in range(4)]
            if j == TILES - 1:
                v = [jnp.where(lane < tail, w, 0.0) for w in v]
            v = [w * fl_ref[F_SEA, j] for w in v]
            if j == 0:
                first = v
            if j == TILES - 1:
                v = [
                    jnp.where(
                        lane < tail,
                        w,
                        jnp.where(lane < tail + 2, pltpu.roll(a, tail, 1), pltpu.roll(w, LANES - tail, 1)),
                    )
                    for w, a in zip(v, first)
                ]
            for i in range(4):
                x_ref[j, pl.ds(base + 8 * i, 8), :] = v[i]
            turned = [pltpu.roll(w, 4, 0) for w in v]
            low = [jnp.where(sub < 4, v[i], turned[i + 1]) for i in (0, 2)]
            high = [jnp.where(sub < 4, turned[i], v[i + 1]) for i in (0, 2)]
            rows = pl.ds(pl.multiple_of(16 * q, 16), 16)
            hs_ref[0, j, rows, :] = jnp.concatenate(low, axis=0).astype(jnp.bfloat16)
            hs_ref[1, j, rows, :] = jnp.concatenate(high, axis=0).astype(jnp.bfloat16)
        return carry

    lax.fori_loop(0, ND // 4, prepare, 0)

    pl.semaphore_wait(barrier, len(OFFSETS) + 2)
    halos = []
    for c in range(CHUNKS):
        for side, b in ((0, south), (1, north)):
            copy = pltpu.make_async_remote_copy(
                src_ref=hs_ref.at[side, pl.ds(PER * c, PER)],
                dst_ref=hr_ref.at[side, pl.ds(PER * c, PER)],
                send_sem=halo_send.at[side, c],
                recv_sem=halo_recv.at[side, c],
                device_id={"band": b},
                device_id_type=MESH,
            )
            copy.start()
            halos.append(copy)

    def along(d, carry):
        base = pl.multiple_of(8 * d, 8)
        cos_d = trig_ref[0, d]
        x = [x_ref[j, pl.ds(base, 8), :] for j in range(TILES)]
        r1 = [pltpu.roll(v, 1, 1) for v in x]
        r2 = [pltpu.roll(v, 2, 1) for v in x]
        l1 = [pltpu.roll(v, LANES - 1, 1) for v in x]
        l2 = [pltpu.roll(v, LANES - 2, 1) for v in x]
        for j in range(TILES):
            before, after = (j - 1) % TILES, (j + 1) % TILES
            behind = jnp.where(lane < 1, r1[before], r1[j])
            far_behind = jnp.where(lane < 2, r2[before], r2[j])
            ahead = jnp.where(lane >= LANES - 1, l1[after], l1[j])
            far_ahead = jnp.where(lane >= LANES - 2, l2[after], l2[j])
            speed = fl_ref[F_CX, j] * cos_d + fl_ref[F_CUR0, j]
            out = x[j] - upwind12(far_behind, behind, x[j], ahead, far_ahead, speed)
            if j == TILES - 1:
                out = jnp.where(lane < tail, out, 0.0)
            adv_ref[j, pl.ds(base, 8), :] = out
        return carry

    lax.fori_loop(0, ND, along, 0)

    keep_dn = (band < bands - 1).astype(jnp.float32)
    keep_up = (band > 0).astype(jnp.float32)
    zero = jnp.zeros((8, LANES), jnp.float32)

    for c in range(CHUNKS):
        halos[2 * c].wait_recv()
        halos[2 * c + 1].wait_recv()

        def across(q, carry):
            rows = pl.ds(pl.multiple_of(16 * q, 16), 16)
            base = pl.multiple_of(32 * q, 32)
            for j in range(PER * c, PER * c + PER):
                dn = hr_ref[0, j, rows, :].astype(jnp.float32) * keep_dn
                up = hr_ref[1, j, rows, :].astype(jnp.float32) * keep_up
                for i in range(4):
                    a, b = dn[8 * (i // 2) : 8 * (i // 2) + 8], up[8 * (i // 2) : 8 * (i // 2) + 8]
                    if i % 2 == 0:
                        h = jnp.where(sub < 4, a, pltpu.roll(b, 4, 0))
                    else:
                        h = jnp.where(sub < 4, pltpu.roll(a, 4, 0), b)
                    here = pl.ds(base + 8 * i, 8)
                    v = x_ref[j, here, :]
                    ahead = pltpu.roll(jnp.where(row == 0, h, v), 6, 0)
                    far_ahead = pltpu.roll(jnp.where(row < 2, h, v), 4, 0)
                    far_behind = pltpu.roll(jnp.where(row < 2, v, h), 4, 0)
                    behind = pltpu.roll(jnp.where(row == 3, h, v), 2, 0)
                    speed = fl_ref[F_CY, j] * trig_ref[1, 4 * q + i] + fl_ref[F_CUR1, j]
                    flux = upwind12(far_behind, behind, v, ahead, far_ahead, speed)
                    adv_ref[j, here, :] = (adv_ref[j, here, :] - flux) * fl_ref[F_SEA, j]
            return carry

        lax.fori_loop(0, ND // 4, across, 0)

        def refract(d, sums):
            cos_d = trig_ref[0, d]
            sin_d = trig_ref[1, d]

            def at(shift):
                return pl.multiple_of(8 * lax.rem(d + (shift + ND), ND), 8)

            places = [at(s) for s in (-2, -1, 0, 1, 2)]
            sums = list(sums)
            for j in range(PER * c, PER * c + PER):
                values = [adv_ref[j, pl.ds(p, 8), :] for p in places]
                speed = fl_ref[F_T0, j] * sin_d - fl_ref[F_T1, j] * cos_d
                out = (values[2] - upwind12(*values, speed)) * fl_ref[F_SEA, j]
                sums[j - PER * c] = sums[j - PER * c] + out * out
                push = fl_ref[F_W0, j] * cos_d + fl_ref[F_W1, j] * sin_d
                t_ref[j, pl.ds(d, 8, stride=ND), :] = out * jnp.exp(jnp.maximum(push - grow_b, 0.0))
            return tuple(sums)

        sums = lax.fori_loop(0, ND, refract, (zero,) * PER)
        for i in range(PER):
            j = PER * c + i
            sq_ref[...] = sums[i] + pltpu.roll(sums[i], 7, 0)
            part_ref[pl.ds(4 * j, 4), :] = sq_ref[pl.ds(0, 4, stride=2), :]

    def reduce_start(axis, src, dst):
        copies = []
        for i in range(1, SIDE):
            o = (0, i) if axis == 0 else (i, 0)
            copy = pltpu.make_async_remote_copy(
                src_ref=src,
                dst_ref=dst.at[i - 1],
                send_sem=sum_send.at[axis, i - 1],
                recv_sem=sum_recv.at[axis, i - 1],
                device_id={"comp": peer(o)},
                device_id_type=MESH,
            )
            copy.start()
            copies.append(copy)
        return copies

    t_rows = t_ref.reshape(GROUPS, COMPS, LANES)

    def step(k, carry):
        tile = tab_ref[AT_TILE + k]
        group = tab_ref[AT_GROUP + k]
        keep = tab_ref[AT_KEEP + k].astype(jnp.float32)
        spot = tab_ref[AT_SPOT + k]
        local = lane + (tab_ref[AT_RANK + tile] - tab_ref[AT_FIRST + group])
        valid = (lane < tab_ref[AT_LEN + tile]) & (local >= 0) & (local < tab_ref[AT_COUNT + group])
        local = jnp.clip(local, 0, LANES - 1)
        idx = jnp.take_along_axis(loc_ref[group], local, axis=1)
        idx_ref[k] = jnp.where(valid, idx, -1)
        parts = []
        for m in range(COMPS // 8):
            data = t_rows[spot, pl.ds(8 * m, 8), :]
            got = jnp.take_along_axis(data, idx, axis=1)
            part = jnp.where(valid, got, carry[m] * keep)
            stage_ref[k, pl.ds(8 * m, 8), :] = part
            parts.append(part)
        return tuple(parts)

    sums_y = reduce_start(0, part_ref, yr_ref)
    carry = lax.fori_loop(0, STEPS // 2, step, (zero,) * (COMPS // 8), unroll=8)
    for copy in sums_y:
        copy.wait()
    for m in range(GROUPS // 8):
        rows = pl.ds(8 * m, 8)
        total_ref[rows, :] = (part_ref[rows, :] + yr_ref[0, rows, :]) + (yr_ref[1, rows, :] + yr_ref[2, rows, :])
    sums_z = reduce_start(1, total_ref, zr_ref)
    lax.fori_loop(STEPS // 2, STEPS, step, carry, unroll=8)
    for copy in sums_z:
        copy.wait()
    for m in range(GROUPS // 8):
        rows = pl.ds(8 * m, 8)
        total = (total_ref[rows, :] + zr_ref[0, rows, :]) + (zr_ref[1, rows, :] + zr_ref[2, rows, :])
        total = jnp.sqrt(total * (1.0 / (BLOCKS * COMPS)) + 1e-6)
        for i in range(8):
            level_ref[8 * m + i] = jnp.broadcast_to(total[i : i + 1], (8, LANES))

    def strengths(k, acc):
        keep = tab_ref[AT_KEEP + k].astype(jnp.float32)
        idx = idx_ref[k]
        got = jnp.take_along_axis(level_ref[tab_ref[AT_SPOT + k]], jnp.maximum(idx, 0), axis=1)
        acc = jnp.where(idx >= 0, got, acc * keep)
        dec_ref[k] = acc
        return acc

    lax.fori_loop(0, STEPS, strengths, zero, unroll=8)

    fade0 = coef_ref[2, FREQS * me]
    fade1 = coef_ref[2, FREQS * me + 1]

    def block(c, store):
        places = [tab_ref[AT_LAST + 3 * c + j] for j in range(3)]
        rows = []
        for j in range(3):
            s = dec_ref[places[j]]
            e0 = jnp.exp(-fade0 * s)
            e1 = jnp.exp(-fade1 * s)
            mixed = jnp.where(sub < 4, e0, e1)
            values = []
            for m in range(COMPS // 8):
                e = e0 if m < 4 else (mixed if m == 4 else e1)
                values.append(stage_ref[places[j], pl.ds(8 * m, 8), :] * e)
            if j < 2:
                rows += values
            else:
                for m in range(5):
                    v = values[m]
                    if m < 4:
                        v = jnp.where(lane < 64, v, pltpu.roll(values[5 + m], 64, 1))
                    rows.append(v)
                rows.append(zero)
        for m in range(PACK // 16):
            store(m, jnp.concatenate(rows[2 * m : 2 * m + 2], axis=0).astype(jnp.bfloat16))

    copies = []
    for i, o in enumerate(OFFSETS):
        other = peer(o)

        def put(m, v):
            sb_ref[i, pl.ds(16 * m, 16), :] = v

        block(other, put)
        copy = pltpu.make_async_remote_copy(
            src_ref=sb_ref.at[i],
            dst_ref=rb_ref.at[me],
            send_sem=send_sem.at[i],
            recv_sem=recv_sem.at[i],
            device_id={"comp": other},
            device_id_type=MESH,
        )
        copy.start()
        copies.append(copy)

    def put_own(m, v):
        rb_ref[me, pl.ds(16 * m, 16), :] = v

    block(me, put_own)
    for copy in halos:
        copy.wait_send()
    for copy in copies:
        copy.wait()


def finish_kernel(rb_ref, out_ref, v_ref):
    def spread(i, carry):
        base = pl.multiple_of(COMPS * i, 8)
        v = rb_ref[i].astype(jnp.float32)
        for j in range(2):
            v_ref[j, pl.ds(base, COMPS), :] = v[COMPS * j : COMPS * (j + 1)]
        v_ref[2, pl.ds(base, 40), :] = v[2 * COMPS : 2 * COMPS + 40]
        v_ref[2, pl.ds(base + 40, 32), :] = pltpu.roll(v[2 * COMPS : 2 * COMPS + 32], 64, 1)
        return carry

    lax.fori_loop(0, BLOCKS, spread, 0, unroll=4)
    for m in range(BLOCKS * COMPS // LANES):
        for j in range(3):
            block = v_ref[j, pl.ds(LANES * m, LANES), :].T.astype(jnp.bfloat16)
            rows = min(LANES, SLOTS - LANES * j)
            out_ref[pl.ds(LANES * j, rows), pl.ds(LANES * m, LANES)] = block[:rows]


def tables(land_mask, counts):
    sea = (land_mask == 0).astype(jnp.float32)
    padded = jnp.pad(sea, ((0, 0), (0, TILES * LANES - NLON))).reshape(GROUPS, LANES)
    lanes = np.arange(LANES)
    upper = (lanes[:, None] <= lanes[None, :]).astype(np.float32)
    inclusive = jnp.dot(padded, upper, preferred_element_type=jnp.float32).astype(jnp.int32)
    local = jnp.sum((inclusive[:, :, None] <= lanes[None, None, :].astype(np.int32)).astype(jnp.int32), axis=1)
    local = jnp.broadcast_to(jnp.minimum(local, LANES - 1)[:, None, :], (GROUPS, 8, LANES))
    count = inclusive[:, LANES - 1]
    groups = np.arange(GROUPS)
    ends = jnp.sum(jnp.where(groups[None, :] <= groups[:, None], count[None, :], 0), axis=1)
    first = ends - count
    blocks = np.arange(BLOCKS)
    starts = jnp.sum(jnp.where(blocks[None, :] < blocks[:, None], counts[None, :], 0), axis=1)
    offset = (np.arange(3) * LANES).astype(np.int32)
    rank = (starts[:, None] + offset[None, :]).reshape(-1)
    length = jnp.clip(counts[:, None] - offset[None, :], 0, LANES).reshape(-1)
    last_rank = rank + jnp.maximum(length, 1) - 1
    low = jnp.minimum(jnp.sum((ends[None, :] <= rank[:, None]).astype(jnp.int32), axis=1), GROUPS - 1)
    high = jnp.minimum(jnp.sum((ends[None, :] <= last_rank[:, None]).astype(jnp.int32), axis=1), GROUPS - 1)
    width = jnp.where(length > 0, high - low + 1, 1)
    tiles = np.arange(3 * BLOCKS)
    stop = jnp.sum(jnp.where(tiles[None, :] <= tiles[:, None], width[None, :], 0), axis=1)
    steps = np.arange(LANES).astype(np.int32)
    tile = jnp.sum((stop[None, :] <= steps[:, None]).astype(jnp.int32), axis=1)
    tile = jnp.minimum(tile, 3 * BLOCKS - 1)
    hit = tile[:, None] == tiles[None, :].astype(np.int32)
    group = steps + jnp.sum(jnp.where(hit, (low - (stop - width))[None, :], 0), axis=1)
    group = jnp.clip(group, 0, GROUPS - 1)
    begin = jnp.sum(jnp.where(hit, (stop - width)[None, :], 0), axis=1)
    keep = (steps > begin).astype(jnp.int32)

    def wide(x):
        return jnp.pad(x.astype(jnp.int32), (0, LANES - x.shape[0]))

    table = jnp.concatenate(
        [tile, group, keep, wide(stop - 1), wide(rank), wide(length), wide(first), wide(count), (group % TILES) * ROWS + group // TILES]
    )
    return table, local


def per_cell(x):
    lead = x.shape[:-2]
    x = jnp.pad(x, ((0, 0),) * (x.ndim - 1) + ((0, TILES * LANES - NLON),))
    x = x.reshape(lead + (ROWS, 1, TILES, LANES))
    x = jnp.broadcast_to(x, lead + (ROWS, FREQS, TILES, LANES))
    x = jnp.moveaxis(x, -2, len(lead))
    return x.reshape(lead + (TILES, 2 * ROWS, LANES))


def body(spectra, depth_class, group_speed, current, depth_slope, wind, land_mask, block_counts):
    comp_index = lax.axis_index("comp")
    band_index = lax.axis_index("band")
    bands = lax.axis_size("band")
    cos_t, sin_t = angles()

    table, local = tables(land_mask, block_counts[0])
    fields = per_cell(
        jnp.concatenate([(land_mask == 0).astype(jnp.float32)[None], current, depth_slope, wind], axis=0)
    )
    depth = per_cell(depth_class)
    own = lax.dynamic_slice_in_dim(group_speed, comp_index * FREQS, FREQS, 1)
    own = jnp.pad(own.T, ((0, 0), (0, LANES - own.shape[0])))
    speeds = jnp.tile(own, (ROWS, 1))
    row_ids = (band_index * ROWS + jnp.arange(ROWS, dtype=jnp.int32)).astype(jnp.float32)
    latitude = (-60.0 + 120.0 * (row_ids + 0.5) / (ROWS * bands)) * (math.pi / 180.0)
    stretch = jnp.broadcast_to(jnp.repeat(1.0 / jnp.cos(latitude), FREQS)[:, None], (8, LANES))

    angular = 2.0 * math.pi * 0.0418 * np.power(1.1, np.arange(BLOCKS * FREQS, dtype=np.float64))
    ratio = angular / angular[-1]
    phase = 9.81 / angular
    coef = np.stack([GROWTH_RATE * ratio / phase, GROWTH_RATE * ratio, DAMPING * ratio]).astype(np.float32)

    vmem = pl.BlockSpec(memory_space=pltpu.VMEM)
    smem = pl.BlockSpec(memory_space=pltpu.SMEM)
    f32, bf16 = jnp.float32, jnp.bfloat16
    dma = pltpu.SemaphoreType.DMA
    rb = pl.pallas_call(
        step_kernel,
        out_shape=jax.ShapeDtypeStruct((BLOCKS, PACK, LANES), bf16),
        in_specs=[smem] * 3 + [vmem] * 6,
        out_specs=vmem,
        scratch_shapes=[
            pltpu.VMEM((TILES, 8 * ND, LANES), f32),
            pltpu.VMEM((TILES, 8 * ND, LANES), f32),
            pltpu.VMEM((TILES, 8 * ND, LANES), f32),
            pltpu.VMEM((STEPS, COMPS, LANES), f32),
            pltpu.VMEM((STEPS, 8, LANES), jnp.int32),
            pltpu.VMEM((STEPS, 8, LANES), f32),
            pltpu.VMEM((9, TILES, 8, LANES), f32),
            pltpu.VMEM((2, TILES, 4 * ND, LANES), bf16),
            pltpu.VMEM((2, TILES, 4 * ND, LANES), bf16),
            pltpu.VMEM((8, LANES), f32),
            pltpu.VMEM((GROUPS, LANES), f32),
            pltpu.VMEM((GROUPS, LANES), f32),
            pltpu.VMEM((GROUPS, 8, LANES), f32),
            pltpu.VMEM((SIDE - 1, GROUPS, LANES), f32),
            pltpu.VMEM((SIDE - 1, GROUPS, LANES), f32),
            pltpu.VMEM((BLOCKS - 1, PACK, LANES), bf16),
            dma((2, CHUNKS)),
            dma((2, CHUNKS)),
            dma((2, SIDE - 1)),
            dma((2, SIDE - 1)),
            dma((BLOCKS - 1,)),
            dma((BLOCKS - 1,)),
        ],
        compiler_params=pltpu.CompilerParams(
            collective_id=0, has_side_effects=True, vmem_limit_bytes=40 * 1024 * 1024
        ),
        name="wave_step",
    )(
        jnp.asarray(np.stack([cos_t, sin_t])),
        table,
        jnp.asarray(coef),
        spectra,
        fields,
        depth,
        speeds,
        stretch,
        local,
    )

    out = pl.pallas_call(
        finish_kernel,
        out_shape=jax.ShapeDtypeStruct((SLOTS, BLOCKS * COMPS), bf16),
        in_specs=[vmem],
        out_specs=vmem,
        scratch_shapes=[pltpu.VMEM((3, BLOCKS * COMPS, LANES), f32)],
        compiler_params=pltpu.CompilerParams(vmem_limit_bytes=16 * 1024 * 1024),
        name="finish",
    )(rb)
    return out.T


def solution(mesh):
    return jax.shard_map(
        body,
        mesh=mesh,
        in_specs=(
            P("comp", None, "band", None),
            P("band", None),
            P(),
            P(None, "band", None),
            P(None, "band", None),
            P(None, "band", None),
            P("band", None),
            P("band", None),
        ),
        out_specs=P(None, ("comp", "band")),
        check_vma=False,
    )
```

time: 71.6 us -> 48.9 us (0.68); the launches traced: 70.3 us -> 48.4 us
  Pallas kernels: 53.7 us -> 39.2 us
  starting transfers between devices: 6.43 us -> 0 us
  waiting for transfers between devices: 1.98 us -> 0 us
  other arithmetic: 5.38 us -> 6.58 us
  matrix products: 0.13 us -> 0.89 us
    pallas_call x3 -> x2, Pallas kernels: 53.7 us -> 39.2 us  [the longest x1 37.6 us: body(): pl.pallas_call(step_kernel, out_shape=jax.ShapeDtypeStruct((BLOCKS, PACK,...]
    ppermute x2 -> x0, starting transfers between devices: 6.43 us -> none  [the longest x1 3.33 us: body(): halo_dn = lax.ppermute(edge(0), 'band', down_pairs)]
    transpose x1 -> x0, other arithmetic: 2.47 us -> none  [edge(): return jnp.transpose(part, (1, 2, 0, 3)).reshape(ND, 2 * FREQS, NLON)]
    ppermute x2 -> x0, waiting for transfers between devices: 1.98 us -> none  [the longest x1 1.86 us: body(): halo_up = lax.ppermute(edge(2), 'band', up_pairs)]
    broadcast_in_dim x1, other arithmetic: 0.03 us -> 0.89 us  [per_cell(): x = jnp.broadcast_to(x, lead + (ROWS, FREQS, TILES, LANES))]
    broadcast_in_dim x3, local copies, waits for them, and re-layouts: 0.11 us -> 0.88 us  [per_cell(): x = jnp.broadcast_to(x, lead + (ROWS, FREQS, TILES, LANES))]
    reduce_sum x1, other arithmetic: 0.11 us -> 0.88 us  [tables(): jnp.sum(jnp.where(blocks[None, :] < blocks[:, None], counts[None, :], 0),...]
    dot_general x1, matrix products: 0.13 us -> 0.89 us  [tables(): jnp.dot(padded, upper, preferred_element_type=jnp.float32).astype(jnp.int32)]
  transfers between devices with their start and end apart: 2 -> 0, of which waited for: 2 -> 0; matrix products, arithmetic and copies ran while one was open for 5% -> 0% of each run, Pallas kernels for 0% -> 0%
where the time goes in v2:
time: 48.9 us; the launch traced here: 48.4 us
  Pallas kernels  39.2 us (80%)
  other arithmetic  6.58 us (13%)
  local copies, waits for them, and re-layouts  1.58 us (3%)
  matrix products  0.89 us (2%)
    pallas_call x1, Pallas kernels, body(): pl.pallas_call(step_kernel, out_shape=jax.ShapeDtypeStruct((BLOCKS, PACK,...  37.6 us
    pallas_call x1, Pallas kernels, body(): pl.pallas_call(finish_kernel, out_shape=jax.ShapeDtypeStruct((SLOTS, BLOC...  1.53 us
    reduce_sum x1, other arithmetic, tables(): jnp.sum((inclusive[:, :, None] <= lanes[None, None, :].astype(np.int32))....  1.23 us

profile of v2, /device:TPU:1, one launch (start us, length us, event | category | flops | bytes accessed | tf_op | source)
XLA Modules:
  0.0 48.4 jit_solution(11907017917206877374)
XLA Ops:
  0.0 0.0 copy-start
  0.0 0.0 copy-start.2
  0.0 0.0 copy-start.3
  0.0 0.0 copy-start.1
  0.1 0.9 %select_reduce_fusion.2 = s32[16]{0:T(128)S(1)} fusion(pred[16,16]{1,0:T(8,128)(4,1)} %constant.89.clone, s32[16]{0:T(128)} %bitcast.22), kind=kLoop, calls=%fused_computation.23 | loop fusion | flops 496 | bytes 384 | tf_op jit(solution)/shard_map/reduce_sum | solution.py:393
  1.0 0.0 copy-done
  1.0 0.1 broadcast_in_dim.109
  1.1 0.1 broadcast_in_dim.110
  1.2 0.1 broadcast_in_dim.111.stretch_ref
  1.2 0.7 %broadcast_add_fusion = (s32[16,3]{1,0:T(8,128)S(1)}, s32[16,3]{1,0:T(8,128)S(1)}) fusion(s32[16]{0:T(128)S(1)} %select_reduce_fusion.2, s32[3]{0:T(128)S(1)} %iota_multiply_fusion, s32[16]{0:T(128)} %bitcast.23), kind=kLoop, calls=%fused_computation.34 | loop fusion | flops 144 | bytes 524 | tf_op jit(solution)/shard_map/add | solution.py:395
  2.0 0.1 add.102
  2.1 0.1 min.64
  2.2 0.7 %pad_bitcast_fusion = s32[4,12,128]{2,0,1:T(4,128)S(1)} fusion(s32[4,1440]{1,0:T(4,128)} %param.21), kind=kLoop, calls=%fused_computation.15 | loop fusion | bytes 47616 | tf_op jit(solution)/shard_map/broadcast_in_dim | solution.py:425
  2.9 0.8 %fusion.8 = (f32[1,4,1440]{2,1,0:T(4,128)S(1)}, bf16[4,1440]{1,0:T(4,128)(2,1)S(1)}) fusion(s32[4,1440]{1,0:T(4,128)} %param.26), kind=kLoop, calls=%fused_computation.50 | loop fusion | flops 17280 | bytes 57600 | tf_op jit(solution)/shard_map/broadcast_in_dim | solution.py:438
  3.7 0.9 %convolution_convert_fusion = s32[48,128]{1,0:T(8,128)S(1)} fusion(bf16[48,128]{1,0:T(8,128)(2,1)S(1)} %reshape.119, bf16[128,128]{1,0:T(8,128)(2,1)} %constant.171), kind=kOutput, calls=%fused_computation.2 | convolution fusion | flops 1579008 | bytes 69632 | tf_op jit(solution)/shard_map/dot_general | solution.py:385
  4.6 0.2 slice_reduce_fusion
  4.8 1.2 %convert_reduce_fusion = s32[48,128]{1,0:T(8,128)S(1)} fusion(s32[48,128]{1,0:T(8,128)S(1)} %convolution_convert_fusion), kind=kLoop, calls=%fused_computation.1 | loop fusion | flops 2353152 | bytes 49152 | tf_op jit(solution)/shard_map/reduce_sum | solution.py:386
  6.0 0.8 %select_reduce_fusion.1 = s32[48]{0:T(128)S(1)} fusion(pred[48,48]{1,0:T(8,128)(4,1)} %constant.88.clone, s32[48]{0:T(128)S(1)} %slice_reduce_fusion), kind=kLoop, calls=%fused_computation.20 | loop fusion | flops 4560 | bytes 2688 | tf_op jit(solution)/shard_map/reduce_sum | solution.py:390
  6.9 0.2 convert_reduce_fusion.2
  7.1 0.8 %select_reduce_fusion = s32[48]{0:T(128)S(1)} fusion(pred[48,48]{1,0:T(8,128)(4,1)} %constant.88.clone, s32[48]{0:T(128)S(1)} %compare_select_fusion), kind=kLoop, calls=%fused_computation.17 | loop fusion | flops 4560 | bytes 2688 | tf_op jit(solution)/shard_map/reduce_sum | solution.py:402
  7.9 0.1 convert_reduce_fusion.1
  8.0 0.1 fusion.4
  8.2 0.9 %fusion = f32[7,4,12,128]{3,1,2,0:T(4,128)S(1)} fusion(f32[2,4,1440]{2,1,0:T(4,128)} %param.25, f32[2,4,1440]{2,1,0:T(4,128)} %param.24, f32[2,4,1440]{2,1,0:T(4,128)} %param.23, f32[1,4,1440]{2,1,0:T(4,128)S(1)} %get-tuple-element.11), kind=kLoop, calls=%fused_computation.4 | loop fusion | flops 344064 | bytes 333312 | tf_op jit(solution)/shard_map/broadcast_in_dim | solution.py:425
  9.1 0.1 broadcast_in_dim.106
  9.2 0.0 copy-done.2
  9.3 0.0 copy-done.3
  9.3 0.0 copy-done.1
  9.3 37.6 %wave_step.1.rb_ref = bf16[16,192,128]{2,1,0:T(8,128)(2,1)S(1)} custom-call(f32[2,36]{1,0:T(2,128)S(1)} %copy-done.3, s32[1152]{0:T(1024)S(1)} %constant_dynamic-update-slice_fusion.tab_ref, f32[3,32]{1,0:T(4,128)S(1)} %copy-done.2, bf16[2,36,4,1440]{3,2,1,0:T(4,128)(2,1)S(1)} %copy-done.1, f32[7,12,8,128]{3,2,1,0:T(8,128)S(1)} %bitcast.19, ...), custom_call_target="tpu_custom_call" | custom-call | tf_op jit(solution)/shard_map/wave_step/pallas_call | solution.py:457
  46.9 1.5 %finish.1 = bf16[315,1152]{1,0:T(8,128)(2,1)} custom-call(bf16[16,192,128]{2,1,0:T(8,128)(2,1)S(1)} %wave_step.1.rb_ref), custom_call_target="tpu_custom_call" | custom-call | tf_op jit(solution)/shard_map/finish/pallas_call | solution.py:502
  (24 shorter events, 0.2 us)
Async XLA Ops:
  0.0 1.0 %copy-start = (f32[64,32]{0,1:T(8,128)S(1)}, f32[64,32]{0,1:T(8,128)}, u32[]{:S(2)}) copy-start(f32[64,32]{0,1:T(8,128)} %param.22) | copy-start | bytes 24580
  0.0 9.2 %copy-start.2 = (f32[3,32]{1,0:T(4,128)S(1)}, f32[3,32]{1,0:T(4,128)}, u32[]{:S(2)}) copy-start(f32[3,32]{1,0:T(4,128)} %constant.94.clone.coef_ref) | copy-start | bytes 1156
  0.0 9.3 %copy-start.3 = (f32[2,36]{1,0:T(2,128)S(1)}, f32[2,36]{1,0:T(2,128)}, u32[]{:S(2)}) copy-start(f32[2,36]{1,0:T(2,128)} %constant.93.clone.trig_ref) | copy-start | bytes 868
  0.0 9.3 %copy-start.1 = (bf16[2,36,4,1440]{3,2,1,0:T(4,128)(2,1)S(1)}, bf16[2,36,4,1440]{3,2,1,0:T(4,128)(2,1)}, u32[]{:S(2)}) copy-start(bf16[2,36,4,1440]{3,2,1,0:T(4,128)(2,1)} %spec_ref.1) | copy-start | bytes 2488324

commit v3 on v2

--- a/solution.py
+++ b/solution.py
@@ -21,6 +21,7 @@
 GROUPS = ROWS * TILES
 BLOCKS = 16
 SLOTS = 315
+DEPTHS = 64
 STEPS = 96
 COMPS = FREQS * ND
 PACK = 192
@@ -28,9 +29,7 @@
 PER = TILES // CHUNKS
 SIDE = 4
 
-AT_TILE, AT_GROUP, AT_KEEP, AT_LAST = 0, 128, 256, 384
-AT_RANK, AT_LEN, AT_FIRST, AT_COUNT = 512, 640, 768, 896
-AT_SPOT = 1024
+AT_SPOT, AT_KEEP, AT_DELTA, AT_LEN, AT_COUNT, AT_LAST = range(6)
 
 (F_SEA, F_CX, F_CY, F_CUR0, F_CUR1, F_T0, F_T1, F_W0, F_W1) = range(9)
 
@@ -57,10 +56,10 @@
 
 
 def step_kernel(
-    trig_ref, tab_ref, coef_ref, spec_ref, fields_ref, depth_ref, gs_ref, stretch_ref, loc_ref,
+    trig_ref, coef_ref, stretch_ref, counts_ref, spec_ref, depth_ref, speed_ref, current_ref, slope_ref, wind_ref, land_ref,
     rb_ref,
-    x_ref, adv_ref, t_ref, stage_ref, idx_ref, dec_ref, fl_ref, hs_ref, hr_ref, sq_ref, part_ref, total_ref, level_ref, yr_ref, zr_ref, sb_ref,
-    halo_send, halo_recv, sum_send, sum_recv, send_sem, recv_sem,
+    gs_ref, raw_ref, cls_ref, flag_ref, tabv_ref, tab_ref, loc_ref, x_ref, adv_ref, t_ref, stage_ref, idx_ref, dec_ref, fl_ref, hs_ref, hr_ref, sq_ref, part_ref, total_ref, level_ref, yr_ref, zr_ref, sb_ref,
+    tab_sem, halo_send, halo_recv, sum_send, sum_recv, send_sem, recv_sem,
 ):
     lane = lax.broadcasted_iota(jnp.int32, (8, LANES), 1)
     sub = lax.broadcasted_iota(jnp.int32, (8, LANES), 0)
@@ -82,24 +81,50 @@
     for o in OFFSETS:
         pl.semaphore_signal(barrier, inc=1, device_id={"comp": peer(o)}, device_id_type=MESH)
 
-    for j in range(TILES):
-        cel = jnp.take_along_axis(gs_ref[...], depth_ref[j], axis=1)
-        sixth = cel * (1.0 / 6.0)
-        fl_ref[F_SEA, j] = fields_ref[0, j]
-        fl_ref[F_CX, j] = sixth * stretch_ref[...]
-        fl_ref[F_CY, j] = sixth
-        fl_ref[F_CUR0, j] = fields_ref[1, j] * (1.0 / 6.0)
-        fl_ref[F_CUR1, j] = fields_ref[2, j] * (1.0 / 6.0)
-        fl_ref[F_T0, j] = (TURNING_SCALE * sixth) * fields_ref[3, j]
-        fl_ref[F_T1, j] = (TURNING_SCALE * sixth) * fields_ref[4, j]
-
     even = lax.rem(sub, 2) == 0
+    even_half = lax.rem(lax.broadcasted_iota(jnp.int32, (8, DEPTHS), 0), 2) == 0
+    gs_ref[:, pl.ds(0, DEPTHS)] = jnp.where(
+        even_half,
+        jnp.broadcast_to(speed_ref[pl.ds(FREQS * me, 1), :], (8, DEPTHS)),
+        jnp.broadcast_to(speed_ref[pl.ds(FREQS * me + 1, 1), :], (8, DEPTHS)),
+    )
     grow_a = jnp.where(even, coef_ref[0, FREQS * me], coef_ref[0, FREQS * me + 1])
     grow_b = jnp.where(even, coef_ref[1, FREQS * me], coef_ref[1, FREQS * me + 1])
-
+    stretch = jnp.where(row == 0, stretch_ref[ROWS * band], stretch_ref[ROWS * band + 1])
+    stretch = jnp.where(row == 2, stretch_ref[ROWS * band + 2], stretch)
+    stretch = jnp.where(row == 3, stretch_ref[ROWS * band + 3], stretch)
+    flag_ref[...] = jnp.zeros((LANES, LANES), jnp.float32)
     for j in range(TILES):
-        fl_ref[F_W0, j] = fields_ref[5, j] * grow_a
-        fl_ref[F_W1, j] = fields_ref[6, j] * grow_a
+        width = LANES if j < TILES - 1 else tail
+        cols = pl.ds(j * LANES, width)
+        sea = (land_ref[:, cols] == 0).astype(jnp.float32)
+        flag_ref[pl.ds(ROWS * j, ROWS), pl.ds(0, width)] = sea
+        parts = [sea] + [ref[i, :, cols] for ref in (current_ref, slope_ref, wind_ref) for i in range(2)]
+        for n, v in enumerate(parts):
+            for f in range(FREQS):
+                raw_ref[j, pl.ds(8 * n + f, 4, stride=2), pl.ds(0, width)] = v
+        v = depth_ref[:, cols]
+        for f in range(FREQS):
+            cls_ref[j, pl.ds(f, 4, stride=2), pl.ds(0, width)] = v
+    for j in range(TILES):
+        def raw(n):
+            v = raw_ref[j, pl.ds(8 * n, 8), :]
+            return v if j < TILES - 1 else jnp.where(lane < tail, v, 0.0)
+
+        cls = cls_ref[j]
+        if j == TILES - 1:
+            cls = jnp.where(lane < tail, cls, 0)
+        cel = jnp.take_along_axis(gs_ref[...], cls, axis=1)
+        sixth = cel * (1.0 / 6.0)
+        fl_ref[F_SEA, j] = raw(0)
+        fl_ref[F_CX, j] = sixth * stretch
+        fl_ref[F_CY, j] = sixth
+        fl_ref[F_CUR0, j] = raw(1) * (1.0 / 6.0)
+        fl_ref[F_CUR1, j] = raw(2) * (1.0 / 6.0)
+        fl_ref[F_T0, j] = (TURNING_SCALE * sixth) * raw(3)
+        fl_ref[F_T1, j] = (TURNING_SCALE * sixth) * raw(4)
+        fl_ref[F_W0, j] = raw(5) * grow_a
+        fl_ref[F_W1, j] = raw(6) * grow_a
 
     def load(d, carry):
         base = pl.multiple_of(8 * d, 8)
@@ -158,6 +183,10 @@
             copy.start()
             halos.append(copy)
 
+    build_tables(counts_ref, flag_ref, tabv_ref, loc_ref)
+    table_copy = pltpu.make_async_copy(tabv_ref, tab_ref, tab_sem)
+    table_copy.start()
+
     def along(d, carry):
         base = pl.multiple_of(8 * d, 8)
         cos_d = trig_ref[0, d]
@@ -179,7 +208,7 @@
             adv_ref[j, pl.ds(base, 8), :] = out
         return carry
 
-    lax.fori_loop(0, ND, along, 0)
+    lax.fori_loop(0, ND, along, 0, unroll=2)
 
     keep_dn = (band < bands - 1).astype(jnp.float32)
     keep_up = (band > 0).astype(jnp.float32)
@@ -232,7 +261,7 @@
                 t_ref[j, pl.ds(d, 8, stride=ND), :] = out * jnp.exp(jnp.maximum(push - grow_b, 0.0))
             return tuple(sums)
 
-        sums = lax.fori_loop(0, ND, refract, (zero,) * PER)
+        sums = lax.fori_loop(0, ND, refract, (zero,) * PER, unroll=3)
         for i in range(PER):
             j = PER * c + i
             sq_ref[...] = sums[i] + pltpu.roll(sums[i], 7, 0)
@@ -257,14 +286,12 @@
     t_rows = t_ref.reshape(GROUPS, COMPS, LANES)
 
     def step(k, carry):
-        tile = tab_ref[AT_TILE + k]
-        group = tab_ref[AT_GROUP + k]
-        keep = tab_ref[AT_KEEP + k].astype(jnp.float32)
-        spot = tab_ref[AT_SPOT + k]
-        local = lane + (tab_ref[AT_RANK + tile] - tab_ref[AT_FIRST + group])
-        valid = (lane < tab_ref[AT_LEN + tile]) & (local >= 0) & (local < tab_ref[AT_COUNT + group])
+        keep = tab_ref[AT_KEEP, k].astype(jnp.float32)
+        spot = tab_ref[AT_SPOT, k]
+        local = lane + tab_ref[AT_DELTA, k]
+        valid = (lane < tab_ref[AT_LEN, k]) & (local >= 0) & (local < tab_ref[AT_COUNT, k])
         local = jnp.clip(local, 0, LANES - 1)
-        idx = jnp.take_along_axis(loc_ref[group], local, axis=1)
+        idx = jnp.take_along_axis(loc_ref[spot], local, axis=1)
         idx_ref[k] = jnp.where(valid, idx, -1)
         parts = []
         for m in range(COMPS // 8):
@@ -276,6 +303,7 @@
         return tuple(parts)
 
     sums_y = reduce_start(0, part_ref, yr_ref)
+    table_copy.wait()
     carry = lax.fori_loop(0, STEPS // 2, step, (zero,) * (COMPS // 8), unroll=8)
     for copy in sums_y:
         copy.wait()
@@ -294,9 +322,9 @@
             level_ref[8 * m + i] = jnp.broadcast_to(total[i : i + 1], (8, LANES))
 
     def strengths(k, acc):
-        keep = tab_ref[AT_KEEP + k].astype(jnp.float32)
+        keep = tab_ref[AT_KEEP, k].astype(jnp.float32)
         idx = idx_ref[k]
-        got = jnp.take_along_axis(level_ref[tab_ref[AT_SPOT + k]], jnp.maximum(idx, 0), axis=1)
+        got = jnp.take_along_axis(level_ref[tab_ref[AT_SPOT, k]], jnp.maximum(idx, 0), axis=1)
         acc = jnp.where(idx >= 0, got, acc * keep)
         dec_ref[k] = acc
         return acc
@@ -307,7 +335,7 @@
     fade1 = coef_ref[2, FREQS * me + 1]
 
     def block(c, store):
-        places = [tab_ref[AT_LAST + 3 * c + j] for j in range(3)]
+        places = [tab_ref[AT_LAST, 3 * c + j] for j in range(3)]
         rows = []
         for j in range(3):
             s = dec_ref[places[j]]
@@ -377,74 +405,88 @@
             out_ref[pl.ds(LANES * j, rows), pl.ds(LANES * m, LANES)] = block[:rows]
 
 
-def tables(land_mask, counts):
-    sea = (land_mask == 0).astype(jnp.float32)
-    padded = jnp.pad(sea, ((0, 0), (0, TILES * LANES - NLON))).reshape(GROUPS, LANES)
-    lanes = np.arange(LANES)
-    upper = (lanes[:, None] <= lanes[None, :]).astype(np.float32)
-    inclusive = jnp.dot(padded, upper, preferred_element_type=jnp.float32).astype(jnp.int32)
-    local = jnp.sum((inclusive[:, :, None] <= lanes[None, None, :].astype(np.int32)).astype(jnp.int32), axis=1)
-    local = jnp.broadcast_to(jnp.minimum(local, LANES - 1)[:, None, :], (GROUPS, 8, LANES))
-    count = inclusive[:, LANES - 1]
-    groups = np.arange(GROUPS)
-    ends = jnp.sum(jnp.where(groups[None, :] <= groups[:, None], count[None, :], 0), axis=1)
-    first = ends - count
-    blocks = np.arange(BLOCKS)
-    starts = jnp.sum(jnp.where(blocks[None, :] < blocks[:, None], counts[None, :], 0), axis=1)
-    offset = (np.arange(3) * LANES).astype(np.int32)
-    rank = (starts[:, None] + offset[None, :]).reshape(-1)
-    length = jnp.clip(counts[:, None] - offset[None, :], 0, LANES).reshape(-1)
-    last_rank = rank + jnp.maximum(length, 1) - 1
-    low = jnp.minimum(jnp.sum((ends[None, :] <= rank[:, None]).astype(jnp.int32), axis=1), GROUPS - 1)
-    high = jnp.minimum(jnp.sum((ends[None, :] <= last_rank[:, None]).astype(jnp.int32), axis=1), GROUPS - 1)
-    width = jnp.where(length > 0, high - low + 1, 1)
-    tiles = np.arange(3 * BLOCKS)
-    stop = jnp.sum(jnp.where(tiles[None, :] <= tiles[:, None], width[None, :], 0), axis=1)
-    steps = np.arange(LANES).astype(np.int32)
-    tile = jnp.sum((stop[None, :] <= steps[:, None]).astype(jnp.int32), axis=1)
-    tile = jnp.minimum(tile, 3 * BLOCKS - 1)
-    hit = tile[:, None] == tiles[None, :].astype(np.int32)
-    group = steps + jnp.sum(jnp.where(hit, (low - (stop - width))[None, :], 0), axis=1)
+def build_tables(counts_ref, flag_ref, tabv_ref, loc_ref):
+    f32, bf16, i32 = jnp.float32, jnp.bfloat16, jnp.int32
+    sub = lax.broadcasted_iota(i32, (LANES, LANES), 0)
+    lanes = lax.broadcasted_iota(i32, (LANES, LANES), 1)
+    lane = lax.broadcasted_iota(i32, (8, LANES), 1)
+
+    def order(i):
+        return jnp.where(i < GROUPS, (i & (ROWS - 1)) * TILES + (i >> 2), i)
+
+    def product(a, b, dims=(((1,), (0,)), ((), ()))):
+        return lax.dot_general(a, b, dims, preferred_element_type=f32)
+
+    upper = (sub <= lanes).astype(f32).astype(bf16)
+    ones = jnp.ones((LANES, LANES), bf16)
+    flags = flag_ref[...].astype(bf16)
+    inclusive = product(flags, upper)
+    count_rows = product(flags, ones)
+    ends = product((order(lanes) <= order(sub)).astype(f32).astype(bf16), count_rows.astype(bf16))[:GROUPS]
+    count = product(ones[:16], flags, (((1,), (1,)), ((), ())))
+    first = product(count.astype(bf16), (order(sub) < order(lanes)).astype(f32).astype(bf16))
+    count, first = count[:8].astype(i32), first[:8].astype(i32)
+
+    wide = lanes[:GROUPS]
+    shift = wide - (inclusive[:GROUPS].astype(i32) - 1)
+    word = jnp.where(flag_ref[pl.ds(0, GROUPS), :] > 0, wide + LANES * shift + LANES * LANES, 0)
+    for k in range(7):
+        bit = LANES << k
+        moved = pltpu.roll(word, LANES - (1 << k), 1)
+        word = jnp.where((moved & bit) != 0, moved, jnp.where((word & bit) != 0, 0, word))
+    word = word & (LANES - 1)
+    for g in range(GROUPS):
+        loc_ref[g] = jnp.broadcast_to(word[g : g + 1], (8, LANES))
+
+    block = (lane * 171) >> 9
+    part = lane - 3 * block
+    size = jnp.zeros((8, LANES), i32)
+    rank = jnp.zeros((8, LANES), i32)
+    start = 0
+    for c in range(BLOCKS):
+        n = counts_ref[0, c]
+        size = jnp.where(block == c, n, size)
+        rank = jnp.where(block == c, start, rank)
+        start = start + n
+    rank = rank + LANES * part
+    length = jnp.clip(size - LANES * part, 0, LANES)
+    real = lane < 3 * BLOCKS
+
+    def groups_before(r):
+        hit = (ends <= r[:1].astype(f32)).astype(f32)
+        return jnp.minimum(jnp.broadcast_to(jnp.sum(hit, axis=0, keepdims=True), (8, LANES)), GROUPS - 1.0)
+
+    low = groups_before(rank)
+    high = groups_before(rank + jnp.maximum(length, 1) - 1)
+    width = jnp.where(real, jnp.where(length > 0, high - low + 1.0, 1.0), 0.0)
+    stop = product(jnp.concatenate([width, width], axis=0).astype(bf16), upper)[:8]
+    begin = stop - width
+    column = jnp.sum(jnp.where(wide <= sub[:GROUPS], width[:1], 0.0), axis=1, keepdims=True)
+    tile = jnp.sum((column <= wide.astype(f32)).astype(f32), axis=0, keepdims=True)
+    tile = jnp.broadcast_to(jnp.minimum(tile, 3 * BLOCKS - 1.0), (8, LANES)).astype(i32)
+
+    def at(values, index):
+        return jnp.take_along_axis(values, index, axis=1)
+
+    group = lane + at((low - begin).astype(i32), tile)
     group = jnp.clip(group, 0, GROUPS - 1)
-    begin = jnp.sum(jnp.where(hit, (stop - width)[None, :], 0), axis=1)
-    keep = (steps > begin).astype(jnp.int32)
-
-    def wide(x):
-        return jnp.pad(x.astype(jnp.int32), (0, LANES - x.shape[0]))
-
-    table = jnp.concatenate(
-        [tile, group, keep, wide(stop - 1), wide(rank), wide(length), wide(first), wide(count), (group % TILES) * ROWS + group // TILES]
+    r = (group * 171) >> 11
+    spot = ROWS * (group - TILES * r) + r
+    tabv_ref[AT_SPOT : AT_SPOT + 1] = spot[:1]
+    tabv_ref[AT_KEEP : AT_KEEP + 1] = (lane > at(begin.astype(i32), tile)).astype(i32)[:1]
+    tabv_ref[AT_DELTA : AT_DELTA + 1] = (at(rank, tile) - at(first, spot))[:1]
+    tabv_ref[AT_LEN : AT_LEN + 1] = at(length, tile)[:1]
+    tabv_ref[AT_COUNT : AT_COUNT + 1] = at(count, spot)[:1]
+    tabv_ref[AT_LAST : AT_LAST + 1] = jnp.clip((stop - 1.0).astype(i32), 0, STEPS - 1)[:1]
+    tabv_ref[AT_LAST + 1 :] = jnp.zeros((7 - AT_LAST, LANES), i32)
+
+
+def body(spectra, depth_class, group_speed, current, depth_slope, wind, land_mask, block_counts):
+    cos_t, sin_t = angles()
+    latitude = (-60.0 + 120.0 * (np.arange(ROWS * lax.axis_size("band")) + 0.5) / (ROWS * lax.axis_size("band"))) * (
+        math.pi / 180.0
     )
-    return table, local
-
-
-def per_cell(x):
-    lead = x.shape[:-2]
-    x = jnp.pad(x, ((0, 0),) * (x.ndim - 1) + ((0, TILES * LANES - NLON),))
-    x = x.reshape(lead + (ROWS, 1, TILES, LANES))
-    x = jnp.broadcast_to(x, lead + (ROWS, FREQS, TILES, LANES))
-    x = jnp.moveaxis(x, -2, len(lead))
-    return x.reshape(lead + (TILES, 2 * ROWS, LANES))
-
-
-def body(spectra, depth_class, group_speed, current, depth_slope, wind, land_mask, block_counts):
-    comp_index = lax.axis_index("comp")
-    band_index = lax.axis_index("band")
-    bands = lax.axis_size("band")
-    cos_t, sin_t = angles()
-
-    table, local = tables(land_mask, block_counts[0])
-    fields = per_cell(
-        jnp.concatenate([(land_mask == 0).astype(jnp.float32)[None], current, depth_slope, wind], axis=0)
-    )
-    depth = per_cell(depth_class)
-    own = lax.dynamic_slice_in_dim(group_speed, comp_index * FREQS, FREQS, 1)
-    own = jnp.pad(own.T, ((0, 0), (0, LANES - own.shape[0])))
-    speeds = jnp.tile(own, (ROWS, 1))
-    row_ids = (band_index * ROWS + jnp.arange(ROWS, dtype=jnp.int32)).astype(jnp.float32)
-    latitude = (-60.0 + 120.0 * (row_ids + 0.5) / (ROWS * bands)) * (math.pi / 180.0)
-    stretch = jnp.broadcast_to(jnp.repeat(1.0 / jnp.cos(latitude), FREQS)[:, None], (8, LANES))
-
+    stretch = (1.0 / np.cos(latitude)).astype(np.float32)
     angular = 2.0 * math.pi * 0.0418 * np.power(1.1, np.arange(BLOCKS * FREQS, dtype=np.float64))
     ratio = angular / angular[-1]
     phase = 9.81 / angular
@@ -457,9 +499,16 @@
     rb = pl.pallas_call(
         step_kernel,
         out_shape=jax.ShapeDtypeStruct((BLOCKS, PACK, LANES), bf16),
-        in_specs=[smem] * 3 + [vmem] * 6,
+        in_specs=[smem] * 4 + [vmem] * 7,
         out_specs=vmem,
         scratch_shapes=[
+            pltpu.VMEM((8, LANES), f32),
+            pltpu.VMEM((TILES, 8 * 7, LANES), f32),
+            pltpu.VMEM((TILES, 8, LANES), jnp.int32),
+            pltpu.VMEM((LANES, LANES), f32),
+            pltpu.VMEM((8, LANES), jnp.int32),
+            pltpu.SMEM((8, LANES), jnp.int32),
+            pltpu.VMEM((GROUPS, 8, LANES), jnp.int32),
             pltpu.VMEM((TILES, 8 * ND, LANES), f32),
             pltpu.VMEM((TILES, 8 * ND, LANES), f32),
             pltpu.VMEM((TILES, 8 * ND, LANES), f32),
@@ -476,6 +525,7 @@
             pltpu.VMEM((SIDE - 1, GROUPS, LANES), f32),
             pltpu.VMEM((SIDE - 1, GROUPS, LANES), f32),
             pltpu.VMEM((BLOCKS - 1, PACK, LANES), bf16),
+            dma,
             dma((2, CHUNKS)),
             dma((2, CHUNKS)),
             dma((2, SIDE - 1)),
@@ -489,14 +539,16 @@
         name="wave_step",
     )(
         jnp.asarray(np.stack([cos_t, sin_t])),
-        table,
         jnp.asarray(coef),
+        jnp.asarray(stretch),
+        block_counts,
         spectra,
-        fields,
-        depth,
-        speeds,
-        stretch,
-        local,
+        depth_class,
+        group_speed.T,
+        current,
+        depth_slope,
+        wind,
+        land_mask,
     )
 
     out = pl.pallas_call(

time: 48.9 us -> 44.9 us (0.918)
  other arithmetic: 6.58 us -> 0 us
  local copies, waits for them, and re-layouts: 1.58 us -> 6.45 us
  Pallas kernels: 39.2 us -> 37.9 us
  matrix products: 0.89 us -> 0 us
    unnamed x13 -> x22, local copies, waits for them, and re-layouts: 0.05 us -> 6.45 us
    reduce_sum x7 -> x0, other arithmetic: 4.08 us -> none  [the longest x1 1.23 us: tables(): jnp.sum((inclusive[:, :, None] <= lanes[None, None, :].astype(np.int32))....]
    broadcast_in_dim x2 -> x0, other arithmetic: 1.64 us -> none  [the longest x1 0.89 us: per_cell(): x = jnp.broadcast_to(x, lead + (ROWS, FREQS, TILES, LANES))]
    pallas_call x1, Pallas kernels: 37.6 us -> 36.4 us  [body(): pl.pallas_call(step_kernel, out_shape=jax.ShapeDtypeStruct((BLOCKS, PACK,...]
    broadcast_in_dim x7 -> x0, local copies, waits for them, and re-layouts: 1.12 us -> none  [the longest x3 0.88 us: per_cell(): x = jnp.broadcast_to(x, lead + (ROWS, FREQS, TILES, LANES))]
    dot_general x1 -> x0, matrix products: 0.89 us -> none  [tables(): jnp.dot(padded, upper, preferred_element_type=jnp.float32).astype(jnp.int32)]
    add x1 -> x0, other arithmetic: 0.73 us -> none  [tables(): rank = (starts[:, None] + offset[None, :]).reshape(-1)]
where the time goes in v3:
time: 44.9 us; the launch traced here: 44.4 us
  Pallas kernels  37.9 us (84%)
  local copies, waits for them, and re-layouts  6.45 us (14%)
    pallas_call x1, Pallas kernels, body(): pl.pallas_call(step_kernel, out_shape=jax.ShapeDtypeStruct((BLOCKS, PACK,...  36.4 us
    unnamed x22, local copies, waits for them, and re-layouts  6.45 us
    pallas_call x1, Pallas kernels, body(): pl.pallas_call(finish_kernel, out_shape=jax.ShapeDtypeStruct((SLOTS, BLOC...  1.53 us

profile of v3, /device:TPU:1, one launch (start us, length us, event | category | flops | bytes accessed | tf_op | source)
XLA Modules:
  0.0 44.4 jit_solution(15749855848527789502)
XLA Ops:
  0.0 0.0 copy-start.10
  0.0 0.0 copy-start.7
  0.0 0.0 copy-start.8
  0.0 0.0 copy-start.9
  0.0 0.6 %copy-done.10 = f32[32]{0:T(128)S(1)} copy-done((f32[32]{0:T(128)S(1)}, f32[32]{0:T(128)}, u32[]{:S(2)}) %copy-start.10) | copy-done | bytes 152
  0.7 0.0 copy-done.7
  0.7 0.0 copy-done.8
  0.7 0.0 copy-done.9
  0.7 0.0 copy-start
  0.7 1.2 %copy-done = bf16[2,36,4,1440]{3,2,1,0:T(4,128)(2,1)S(1)} copy-done((bf16[2,36,4,1440]{3,2,1,0:T(4,128)(2,1)S(1)}, bf16[2,36,4,1440]{3,2,1,0:T(4,128)(2,1)}, u32[]{:S(2)}) %copy-start) | copy-done | bytes 829464
  1.9 0.0 copy-start.1
  1.9 0.8 %copy-done.1 = f32[2,4,1440]{2,1,0:T(4,128)S(1)} copy-done((f32[2,4,1440]{2,1,0:T(4,128)S(1)}, f32[2,4,1440]{2,1,0:T(4,128)}, u32[]{:S(2)}) %copy-start.1) | copy-done | bytes 46104
  2.7 0.0 copy-start.2
  2.7 0.8 %copy-done.2 = f32[2,4,1440]{2,1,0:T(4,128)S(1)} copy-done((f32[2,4,1440]{2,1,0:T(4,128)S(1)}, f32[2,4,1440]{2,1,0:T(4,128)}, u32[]{:S(2)}) %copy-start.2) | copy-done | bytes 46104
  3.5 0.0 copy-start.3
  3.5 0.8 %copy-done.3 = f32[2,4,1440]{2,1,0:T(4,128)S(1)} copy-done((f32[2,4,1440]{2,1,0:T(4,128)S(1)}, f32[2,4,1440]{2,1,0:T(4,128)}, u32[]{:S(2)}) %copy-start.3) | copy-done | bytes 46104
  4.3 0.0 copy-start.4
  4.3 0.7 %copy-done.4 = s32[4,1440]{1,0:T(4,128)S(1)} copy-done((s32[4,1440]{1,0:T(4,128)S(1)}, s32[4,1440]{1,0:T(4,128)}, u32[]{:S(2)}) %copy-start.4) | copy-done | bytes 23064
  5.0 0.0 copy-start.5
  5.0 0.7 %copy-done.5 = s32[4,1440]{1,0:T(4,128)S(1)} copy-done((s32[4,1440]{1,0:T(4,128)S(1)}, s32[4,1440]{1,0:T(4,128)}, u32[]{:S(2)}) %copy-start.5) | copy-done | bytes 23064
  5.8 0.0 copy-start.6
  5.8 0.7 %copy-done.6 = f32[64,32]{0,1:T(8,128)S(1)} copy-done((f32[64,32]{0,1:T(8,128)S(1)}, f32[64,32]{0,1:T(8,128)}, u32[]{:S(2)}) %copy-start.6) | copy-done | bytes 8216
  6.5 36.4 %wave_step.1.rb_ref = bf16[16,192,128]{2,1,0:T(8,128)(2,1)S(1)} custom-call(f32[2,36]{1,0:T(2,128)S(1)} %copy-done.8, f32[3,32]{1,0:T(4,128)S(1)} %copy-done.7, f32[32]{0:T(128)S(1)} %copy-done.10, s32[1,16]{1,0:T(1,128)S(1)} %copy-done.9, bf16[2,36,4,1440]{3,2,1,0:T(4,128)(2,1)S(1)} %copy-done, s32[4,1440]{1,0:T(4,128)S(1)} %copy-done.4, ...), custom_call_target="tpu_custom_call" | custom-call | tf_op jit(solution)/shard_map/wave_step/pallas_call | solution.py:499
  42.8 1.5 %finish.1 = bf16[315,1152]{1,0:T(8,128)(2,1)} custom-call(bf16[16,192,128]{2,1,0:T(8,128)(2,1)S(1)} %wave_step.1.rb_ref), custom_call_target="tpu_custom_call" | custom-call | tf_op jit(solution)/shard_map/finish/pallas_call | solution.py:554
Async XLA Ops:
  0.0 0.7 %copy-start.10 = (f32[32]{0:T(128)S(1)}, f32[32]{0:T(128)}, u32[]{:S(2)}) copy-start(f32[32]{0:T(128)} %constant.8.clone.stretch_ref) | copy-start | bytes 388
  0.0 0.7 %copy-start.7 = (f32[3,32]{1,0:T(4,128)S(1)}, f32[3,32]{1,0:T(4,128)}, u32[]{:S(2)}) copy-start(f32[3,32]{1,0:T(4,128)} %constant.7.clone.coef_ref) | copy-start | bytes 1156
  0.0 0.7 %copy-start.8 = (f32[2,36]{1,0:T(2,128)S(1)}, f32[2,36]{1,0:T(2,128)}, u32[]{:S(2)}) copy-start(f32[2,36]{1,0:T(2,128)} %constant.6.clone.trig_ref) | copy-start | bytes 868
  0.0 0.7 %copy-start.9 = (s32[1,16]{1,0:T(1,128)S(1)}, s32[1,16]{1,0:T(1,128)}, u32[]{:S(2)}) copy-start(s32[1,16]{1,0:T(1,128)} %counts_ref.1) | copy-start | bytes 196
  0.7 1.2 %copy-start = (bf16[2,36,4,1440]{3,2,1,0:T(4,128)(2,1)S(1)}, bf16[2,36,4,1440]{3,2,1,0:T(4,128)(2,1)}, u32[]{:S(2)}) copy-start(bf16[2,36,4,1440]{3,2,1,0:T(4,128)(2,1)} %spec_ref.1) | copy-start | bytes 2488324
  1.9 0.8 %copy-start.1 = (f32[2,4,1440]{2,1,0:T(4,128)S(1)}, f32[2,4,1440]{2,1,0:T(4,128)}, u32[]{:S(2)}) copy-start(f32[2,4,1440]{2,1,0:T(4,128)} %current_ref.1) | copy-start | bytes 138244
  2.7 0.8 %copy-start.2 = (f32[2,4,1440]{2,1,0:T(4,128)S(1)}, f32[2,4,1440]{2,1,0:T(4,128)}, u32[]{:S(2)}) copy-start(f32[2,4,1440]{2,1,0:T(4,128)} %slope_ref.1) | copy-start | bytes 138244
  3.5 0.8 %copy-start.3 = (f32[2,4,1440]{2,1,0:T(4,128)S(1)}, f32[2,4,1440]{2,1,0:T(4,128)}, u32[]{:S(2)}) copy-start(f32[2,4,1440]{2,1,0:T(4,128)} %wind_ref.1) | copy-start | bytes 138244
  4.3 0.7 %copy-start.4 = (s32[4,1440]{1,0:T(4,128)S(1)}, s32[4,1440]{1,0:T(4,128)}, u32[]{:S(2)}) copy-start(s32[4,1440]{1,0:T(4,128)} %depth_ref.1) | copy-start | bytes 69124
  5.0 0.7 %copy-start.5 = (s32[4,1440]{1,0:T(4,128)S(1)}, s32[4,1440]{1,0:T(4,128)}, u32[]{:S(2)}) copy-start(s32[4,1440]{1,0:T(4,128)} %land_ref.1) | copy-start | bytes 69124
  5.8 0.7 %copy-start.6 = (f32[64,32]{0,1:T(8,128)S(1)}, f32[64,32]{0,1:T(8,128)}, u32[]{:S(2)}) copy-start(f32[64,32]{0,1:T(8,128)} %param.13) | copy-start | bytes 24580

commit v4 on v3

--- a/solution.py
+++ b/solution.py
@@ -31,7 +31,7 @@
 
 AT_SPOT, AT_KEEP, AT_DELTA, AT_LEN, AT_COUNT, AT_LAST = range(6)
 
-(F_SEA, F_CX, F_CY, F_CUR0, F_CUR1, F_T0, F_T1, F_W0, F_W1) = range(9)
+(F_SEA, F_CX, F_CY, F_CUR0, F_CUR1, F_T0, F_T1) = range(7)
 
 MESH = pl.DeviceIdType.MESH
 
@@ -56,11 +56,32 @@
 
 
 def step_kernel(
-    trig_ref, coef_ref, stretch_ref, counts_ref, spec_ref, depth_ref, speed_ref, current_ref, slope_ref, wind_ref, land_ref,
+    scalars_hbm, compass_hbm, counts_hbm, spec_hbm, depth_hbm, speed_hbm, current_hbm, slope_hbm, wind_hbm, land_hbm,
     rb_ref,
-    gs_ref, raw_ref, cls_ref, flag_ref, tabv_ref, tab_ref, loc_ref, x_ref, adv_ref, t_ref, stage_ref, idx_ref, dec_ref, fl_ref, hs_ref, hr_ref, sq_ref, part_ref, total_ref, level_ref, yr_ref, zr_ref, sb_ref,
-    tab_sem, halo_send, halo_recv, sum_send, sum_recv, send_sem, recv_sem,
+    scalars_ref, compass_ref, counts_ref, spec_ref, depth_ref, speed_ref, current_ref, slope_ref, wind_ref, land_ref,
+    gust_ref, gusts_ref,
+    gs_ref, raw_ref, cls_ref, flag_ref, tabv_ref, tab_ref, loc_ref, x_ref, adv_ref, t_ref, stage_ref, grown_ref, idx_ref, dec_ref, fl_ref, hs_ref, hr_ref, sq_ref, part_ref, total_ref, level_ref, yr_ref, zr_ref, sb_ref,
+    in_sem, tab_sem, halo_send, halo_recv, sum_send, sum_recv, send_sem, recv_sem,
 ):
+    arrivals = [
+        pltpu.make_async_copy(src, dst, in_sem.at[i])
+        for i, (src, dst) in enumerate(
+            [
+                (land_hbm, land_ref),
+                (spec_hbm, spec_ref),
+                (scalars_hbm, scalars_ref),
+                (speed_hbm, speed_ref),
+                (depth_hbm, depth_ref),
+                (current_hbm, current_ref),
+                (slope_hbm, slope_ref),
+                (wind_hbm, wind_ref),
+                (counts_hbm, counts_ref),
+                (compass_hbm, compass_ref),
+            ]
+        )
+    ]
+    for copy in arrivals:
+        copy.start()
     lane = lax.broadcasted_iota(jnp.int32, (8, LANES), 1)
     sub = lax.broadcasted_iota(jnp.int32, (8, LANES), 0)
     row = sub // 2
@@ -81,25 +102,29 @@
     for o in OFFSETS:
         pl.semaphore_signal(barrier, inc=1, device_id={"comp": peer(o)}, device_id_type=MESH)
 
-    even = lax.rem(sub, 2) == 0
+    for copy in arrivals:
+        copy.wait()
+
     even_half = lax.rem(lax.broadcasted_iota(jnp.int32, (8, DEPTHS), 0), 2) == 0
     gs_ref[:, pl.ds(0, DEPTHS)] = jnp.where(
         even_half,
         jnp.broadcast_to(speed_ref[pl.ds(FREQS * me, 1), :], (8, DEPTHS)),
         jnp.broadcast_to(speed_ref[pl.ds(FREQS * me + 1, 1), :], (8, DEPTHS)),
     )
-    grow_a = jnp.where(even, coef_ref[0, FREQS * me], coef_ref[0, FREQS * me + 1])
-    grow_b = jnp.where(even, coef_ref[1, FREQS * me], coef_ref[1, FREQS * me + 1])
-    stretch = jnp.where(row == 0, stretch_ref[ROWS * band], stretch_ref[ROWS * band + 1])
-    stretch = jnp.where(row == 2, stretch_ref[ROWS * band + 2], stretch)
-    stretch = jnp.where(row == 3, stretch_ref[ROWS * band + 3], stretch)
+    stretch = jnp.where(row == 0, scalars_ref[5, ROWS * band], scalars_ref[5, ROWS * band + 1])
+    stretch = jnp.where(row == 2, scalars_ref[5, ROWS * band + 2], stretch)
+    stretch = jnp.where(row == 3, scalars_ref[5, ROWS * band + 3], stretch)
     flag_ref[...] = jnp.zeros((LANES, LANES), jnp.float32)
     for j in range(TILES):
         width = LANES if j < TILES - 1 else tail
         cols = pl.ds(j * LANES, width)
         sea = (land_ref[:, cols] == 0).astype(jnp.float32)
         flag_ref[pl.ds(ROWS * j, ROWS), pl.ds(0, width)] = sea
-        parts = [sea] + [ref[i, :, cols] for ref in (current_ref, slope_ref, wind_ref) for i in range(2)]
+        for i in range(2):
+            gust = wind_ref[i, :, cols]
+            for r in range(ROWS):
+                gust_ref[ROWS * j + r, i : i + 1, pl.ds(0, width)] = gust[r : r + 1]
+        parts = [sea] + [ref[i, :, cols] for ref in (current_ref, slope_ref) for i in range(2)]
         for n, v in enumerate(parts):
             for f in range(FREQS):
                 raw_ref[j, pl.ds(8 * n + f, 4, stride=2), pl.ds(0, width)] = v
@@ -123,8 +148,6 @@
         fl_ref[F_CUR1, j] = raw(2) * (1.0 / 6.0)
         fl_ref[F_T0, j] = (TURNING_SCALE * sixth) * raw(3)
         fl_ref[F_T1, j] = (TURNING_SCALE * sixth) * raw(4)
-        fl_ref[F_W0, j] = raw(5) * grow_a
-        fl_ref[F_W1, j] = raw(6) * grow_a
 
     def load(d, carry):
         base = pl.multiple_of(8 * d, 8)
@@ -189,7 +212,7 @@
 
     def along(d, carry):
         base = pl.multiple_of(8 * d, 8)
-        cos_d = trig_ref[0, d]
+        cos_d = scalars_ref[0, d]
         x = [x_ref[j, pl.ds(base, 8), :] for j in range(TILES)]
         r1 = [pltpu.roll(v, 1, 1) for v in x]
         r2 = [pltpu.roll(v, 2, 1) for v in x]
@@ -236,16 +259,16 @@
                     far_ahead = pltpu.roll(jnp.where(row < 2, h, v), 4, 0)
                     far_behind = pltpu.roll(jnp.where(row < 2, v, h), 4, 0)
                     behind = pltpu.roll(jnp.where(row == 3, h, v), 2, 0)
-                    speed = fl_ref[F_CY, j] * trig_ref[1, 4 * q + i] + fl_ref[F_CUR1, j]
+                    speed = fl_ref[F_CY, j] * scalars_ref[1, 4 * q + i] + fl_ref[F_CUR1, j]
                     flux = upwind12(far_behind, behind, v, ahead, far_ahead, speed)
                     adv_ref[j, here, :] = (adv_ref[j, here, :] - flux) * fl_ref[F_SEA, j]
             return carry
 
-        lax.fori_loop(0, ND // 4, across, 0)
+        lax.fori_loop(0, ND // 4, across, 0, unroll=1)
 
         def refract(d, sums):
-            cos_d = trig_ref[0, d]
-            sin_d = trig_ref[1, d]
+            cos_d = scalars_ref[0, d]
+            sin_d = scalars_ref[1, d]
 
             def at(shift):
                 return pl.multiple_of(8 * lax.rem(d + (shift + ND), ND), 8)
@@ -257,8 +280,7 @@
                 speed = fl_ref[F_T0, j] * sin_d - fl_ref[F_T1, j] * cos_d
                 out = (values[2] - upwind12(*values, speed)) * fl_ref[F_SEA, j]
                 sums[j - PER * c] = sums[j - PER * c] + out * out
-                push = fl_ref[F_W0, j] * cos_d + fl_ref[F_W1, j] * sin_d
-                t_ref[j, pl.ds(d, 8, stride=ND), :] = out * jnp.exp(jnp.maximum(push - grow_b, 0.0))
+                t_ref[j, pl.ds(d, 8, stride=ND), :] = out
             return tuple(sums)
 
         sums = lax.fori_loop(0, ND, refract, (zero,) * PER, unroll=3)
@@ -300,18 +322,44 @@
             part = jnp.where(valid, got, carry[m] * keep)
             stage_ref[k, pl.ds(8 * m, 8), :] = part
             parts.append(part)
-        return tuple(parts)
+        gust = jnp.where(valid, jnp.take_along_axis(gust_ref[spot], idx, axis=1), carry[COMPS // 8])
+        gusts_ref[k] = gust
+        return tuple(parts) + (gust,)
 
     sums_y = reduce_start(0, part_ref, yr_ref)
     table_copy.wait()
-    carry = lax.fori_loop(0, STEPS // 2, step, (zero,) * (COMPS // 8), unroll=8)
+    lax.fori_loop(0, STEPS, step, (zero,) * (COMPS // 8 + 1), unroll=8)
     for copy in sums_y:
         copy.wait()
     for m in range(GROUPS // 8):
         rows = pl.ds(8 * m, 8)
         total_ref[rows, :] = (part_ref[rows, :] + yr_ref[0, rows, :]) + (yr_ref[1, rows, :] + yr_ref[2, rows, :])
     sums_z = reduce_start(1, total_ref, zr_ref)
-    lax.fori_loop(STEPS // 2, STEPS, step, carry, unroll=8)
+
+    def by_row(q):
+        low, high = scalars_ref[q, FREQS * me], scalars_ref[q, FREQS * me + 1]
+        mixed = jnp.where(sub < 4, low, high)
+        return [low if m < 4 else (mixed if m == 4 else high) for m in range(COMPS // 8)]
+
+    rise, calm = by_row(2), by_row(3)
+    for i in range(2):
+        for m in range(COMPS // 8):
+            rows = pl.ds(8 * m, 8)
+            compass_ref[i, rows, :] = compass_ref[i, rows, :] * rise[m]
+
+    def grow(c, carry):
+        for j in range(3):
+            k = tab_ref[AT_LAST, 3 * c + j]
+            gust = gusts_ref[k]
+            east = jnp.broadcast_to(gust[0:1], (8, LANES))
+            north = jnp.broadcast_to(gust[1:2], (8, LANES))
+            for m in range(COMPS // 8):
+                rows = pl.ds(8 * m, 8)
+                push = east * compass_ref[0, rows, :] + north * compass_ref[1, rows, :]
+                grown_ref[3 * c + j, rows, :] = stage_ref[k, rows, :] * jnp.exp(jnp.maximum(push - calm[m], 0.0))
+        return carry
+
+    lax.fori_loop(0, BLOCKS, grow, 0)
     for copy in sums_z:
         copy.wait()
     for m in range(GROUPS // 8):
@@ -329,10 +377,10 @@
         dec_ref[k] = acc
         return acc
 
-    lax.fori_loop(0, STEPS, strengths, zero, unroll=8)
-
-    fade0 = coef_ref[2, FREQS * me]
-    fade1 = coef_ref[2, FREQS * me + 1]
+    lax.fori_loop(0, STEPS, strengths, zero, unroll=16)
+
+    fade0 = scalars_ref[4, FREQS * me]
+    fade1 = scalars_ref[4, FREQS * me + 1]
 
     def block(c, store):
         places = [tab_ref[AT_LAST, 3 * c + j] for j in range(3)]
@@ -345,7 +393,7 @@
             values = []
             for m in range(COMPS // 8):
                 e = e0 if m < 4 else (mixed if m == 4 else e1)
-                values.append(stage_ref[places[j], pl.ds(8 * m, 8), :] * e)
+                values.append(grown_ref[3 * c + j, pl.ds(8 * m, 8), :] * e)
             if j < 2:
                 rows += values
             else:
@@ -492,18 +540,36 @@
     phase = 9.81 / angular
     coef = np.stack([GROWTH_RATE * ratio / phase, GROWTH_RATE * ratio, DAMPING * ratio]).astype(np.float32)
 
+    scalars = np.zeros((8, LANES), np.float32)
+    scalars[0, :ND], scalars[1, :ND] = cos_t, sin_t
+    scalars[2:5, : BLOCKS * FREQS] = coef
+    scalars[5, : stretch.size] = stretch
+    compass = np.stack([np.tile(cos_t, FREQS), np.tile(sin_t, FREQS)])
+    compass = np.ascontiguousarray(np.broadcast_to(compass[:, :, None], (2, COMPS, LANES)))
+
     vmem = pl.BlockSpec(memory_space=pltpu.VMEM)
-    smem = pl.BlockSpec(memory_space=pltpu.SMEM)
     f32, bf16 = jnp.float32, jnp.bfloat16
     dma = pltpu.SemaphoreType.DMA
     rb = pl.pallas_call(
         step_kernel,
         out_shape=jax.ShapeDtypeStruct((BLOCKS, PACK, LANES), bf16),
-        in_specs=[smem] * 4 + [vmem] * 7,
+        in_specs=[pl.BlockSpec(memory_space=pltpu.HBM)] * 10,
         out_specs=vmem,
         scratch_shapes=[
+            pltpu.SMEM((8, LANES), f32),
+            pltpu.VMEM((2, COMPS, LANES), f32),
+            pltpu.SMEM(block_counts.shape, jnp.int32),
+            pltpu.VMEM(spectra.shape, bf16),
+            pltpu.VMEM(depth_class.shape, jnp.int32),
+            pltpu.VMEM(group_speed.shape[::-1], f32),
+            pltpu.VMEM(current.shape, f32),
+            pltpu.VMEM(depth_slope.shape, f32),
+            pltpu.VMEM(wind.shape, f32),
+            pltpu.VMEM(land_mask.shape, jnp.int32),
+            pltpu.VMEM((GROUPS, 8, LANES), f32),
+            pltpu.VMEM((STEPS, 8, LANES), f32),
             pltpu.VMEM((8, LANES), f32),
-            pltpu.VMEM((TILES, 8 * 7, LANES), f32),
+            pltpu.VMEM((TILES, 8 * 5, LANES), f32),
             pltpu.VMEM((TILES, 8, LANES), jnp.int32),
             pltpu.VMEM((LANES, LANES), f32),
             pltpu.VMEM((8, LANES), jnp.int32),
@@ -513,9 +579,10 @@
             pltpu.VMEM((TILES, 8 * ND, LANES), f32),
             pltpu.VMEM((TILES, 8 * ND, LANES), f32),
             pltpu.VMEM((STEPS, COMPS, LANES), f32),
+            pltpu.VMEM((3 * BLOCKS, COMPS, LANES), f32),
             pltpu.VMEM((STEPS, 8, LANES), jnp.int32),
             pltpu.VMEM((STEPS, 8, LANES), f32),
-            pltpu.VMEM((9, TILES, 8, LANES), f32),
+            pltpu.VMEM((7, TILES, 8, LANES), f32),
             pltpu.VMEM((2, TILES, 4 * ND, LANES), bf16),
             pltpu.VMEM((2, TILES, 4 * ND, LANES), bf16),
             pltpu.VMEM((8, LANES), f32),
@@ -525,6 +592,7 @@
             pltpu.VMEM((SIDE - 1, GROUPS, LANES), f32),
             pltpu.VMEM((SIDE - 1, GROUPS, LANES), f32),
             pltpu.VMEM((BLOCKS - 1, PACK, LANES), bf16),
+            dma((10,)),
             dma,
             dma((2, CHUNKS)),
             dma((2, CHUNKS)),
@@ -538,9 +606,8 @@
         ),
         name="wave_step",
     )(
-        jnp.asarray(np.stack([cos_t, sin_t])),
-        jnp.asarray(coef),
-        jnp.asarray(stretch),
+        jnp.asarray(scalars),
+        jnp.asarray(compass),
         block_counts,
         spectra,
         depth_class,

time: 44.9 us -> 46.6 us (1.038)
  local copies, waits for them, and re-layouts: 6.45 us -> 7.98 us
    unnamed x22 -> x20, local copies, waits for them, and re-layouts: 6.45 us -> 7.98 us
where the time goes in v4:
time: 46.6 us; the launch traced here: 46 us
  Pallas kernels  38 us (82%)
  local copies, waits for them, and re-layouts  7.98 us (17%)
    pallas_call x1, Pallas kernels, body(): pl.pallas_call(step_kernel, out_shape=jax.ShapeDtypeStruct((BLOCKS, PACK,...  36.5 us
    unnamed x20, local copies, waits for them, and re-layouts  7.98 us
    pallas_call x1, Pallas kernels, body(): pl.pallas_call(finish_kernel, out_shape=jax.ShapeDtypeStruct((SLOTS, BLOC...  1.53 us

profile of v4, /device:TPU:1, one launch (start us, length us, event | category | flops | bytes accessed | tf_op | source)
XLA Modules:
  0.0 46.0 jit_solution(13400865440362353143)
XLA Ops:
  0.0 0.0 copy-start.9
  0.0 0.7 %copy-done.9 = s32[1,16]{1,0:T(1,128)S(1)} copy-done((s32[1,16]{1,0:T(1,128)S(1)}, s32[1,16]{1,0:T(1,128)}, u32[]{:S(2)}) %copy-start.9) | copy-done | bytes 88
  0.7 0.0 copy-start
  0.7 1.2 %copy-done = bf16[2,36,4,1440]{3,2,1,0:T(4,128)(2,1)S(1)} copy-done((bf16[2,36,4,1440]{3,2,1,0:T(4,128)(2,1)S(1)}, bf16[2,36,4,1440]{3,2,1,0:T(4,128)(2,1)}, u32[]{:S(2)}) %copy-start) | copy-done | bytes 829464
  1.8 0.0 copy-start.1
  1.8 0.9 %copy-done.1 = f32[2,72,128]{2,1,0:T(8,128)S(1)} copy-done((f32[2,72,128]{2,1,0:T(8,128)S(1)}, f32[2,72,128]{2,1,0:T(8,128)}, u32[]{:S(2)}) %copy-start.1) | copy-done | bytes 73752
  2.7 0.0 copy-start.2
  2.7 0.8 %copy-done.2 = f32[2,4,1440]{2,1,0:T(4,128)S(1)} copy-done((f32[2,4,1440]{2,1,0:T(4,128)S(1)}, f32[2,4,1440]{2,1,0:T(4,128)}, u32[]{:S(2)}) %copy-start.2) | copy-done | bytes 46104
  3.5 0.0 copy-start.3
  3.5 0.8 %copy-done.3 = f32[2,4,1440]{2,1,0:T(4,128)S(1)} copy-done((f32[2,4,1440]{2,1,0:T(4,128)S(1)}, f32[2,4,1440]{2,1,0:T(4,128)}, u32[]{:S(2)}) %copy-start.3) | copy-done | bytes 46104
  4.3 0.0 copy-start.4
  4.3 0.8 %copy-done.4 = f32[2,4,1440]{2,1,0:T(4,128)S(1)} copy-done((f32[2,4,1440]{2,1,0:T(4,128)S(1)}, f32[2,4,1440]{2,1,0:T(4,128)}, u32[]{:S(2)}) %copy-start.4) | copy-done | bytes 46104
  5.1 0.0 copy-start.5
  5.1 0.7 %copy-done.5 = s32[4,1440]{1,0:T(4,128)S(1)} copy-done((s32[4,1440]{1,0:T(4,128)S(1)}, s32[4,1440]{1,0:T(4,128)}, u32[]{:S(2)}) %copy-start.5) | copy-done | bytes 23064
  5.8 0.0 copy-start.6
  5.8 0.7 %copy-done.6 = s32[4,1440]{1,0:T(4,128)S(1)} copy-done((s32[4,1440]{1,0:T(4,128)S(1)}, s32[4,1440]{1,0:T(4,128)}, u32[]{:S(2)}) %copy-start.6) | copy-done | bytes 23064
  6.6 0.0 copy-start.7
  6.6 0.7 %copy-done.7 = f32[64,32]{0,1:T(8,128)S(1)} copy-done((f32[64,32]{0,1:T(8,128)S(1)}, f32[64,32]{0,1:T(8,128)}, u32[]{:S(2)}) %copy-start.7) | copy-done | bytes 8216
  7.3 0.0 copy-start.8
  7.3 0.7 %copy-done.8 = f32[8,128]{1,0:T(8,128)S(1)} copy-done((f32[8,128]{1,0:T(8,128)S(1)}, f32[8,128]{1,0:T(8,128)}, u32[]{:S(2)}) %copy-start.8) | copy-done | bytes 4120
  8.0 36.5 %wave_step.1.rb_ref = bf16[16,192,128]{2,1,0:T(8,128)(2,1)S(1)} custom-call(f32[8,128]{1,0:T(8,128)S(1)} %copy-done.8, f32[2,72,128]{2,1,0:T(8,128)S(1)} %copy-done.1, s32[1,16]{1,0:T(1,128)S(1)} %copy-done.9, bf16[2,36,4,1440]{3,2,1,0:T(4,128)(2,1)S(1)} %copy-done, s32[4,1440]{1,0:T(4,128)S(1)} %copy-done.5, f32[32,64]{1,0:T(8,128)S(1)} %bitcast.2, ...), custom_call_target="tpu_custom_call" | custom-call | tf_op jit(solution)/shard_map/wave_step/pallas_call | solution.py:553
  44.5 1.5 %finish.1 = bf16[315,1152]{1,0:T(8,128)(2,1)} custom-call(bf16[16,192,128]{2,1,0:T(8,128)(2,1)S(1)} %wave_step.1.rb_ref), custom_call_target="tpu_custom_call" | custom-call | tf_op jit(solution)/shard_map/finish/pallas_call | solution.py:621
Async XLA Ops:
  0.0 0.7 %copy-start.9 = (s32[1,16]{1,0:T(1,128)S(1)}, s32[1,16]{1,0:T(1,128)}, u32[]{:S(2)}) copy-start(s32[1,16]{1,0:T(1,128)} %counts_hbm.1) | copy-start | bytes 196
  0.7 1.2 %copy-start = (bf16[2,36,4,1440]{3,2,1,0:T(4,128)(2,1)S(1)}, bf16[2,36,4,1440]{3,2,1,0:T(4,128)(2,1)}, u32[]{:S(2)}) copy-start(bf16[2,36,4,1440]{3,2,1,0:T(4,128)(2,1)} %spec_hbm.1) | copy-start | bytes 2488324
  1.8 0.9 %copy-start.1 = (f32[2,72,128]{2,1,0:T(8,128)S(1)}, f32[2,72,128]{2,1,0:T(8,128)}, u32[]{:S(2)}) copy-start(f32[2,72,128]{2,1,0:T(8,128)} %constant.5.clone.compass_hbm) | copy-start | bytes 221188
  2.7 0.8 %copy-start.2 = (f32[2,4,1440]{2,1,0:T(4,128)S(1)}, f32[2,4,1440]{2,1,0:T(4,128)}, u32[]{:S(2)}) copy-start(f32[2,4,1440]{2,1,0:T(4,128)} %current_hbm.1) | copy-start | bytes 138244
  3.5 0.8 %copy-start.3 = (f32[2,4,1440]{2,1,0:T(4,128)S(1)}, f32[2,4,1440]{2,1,0:T(4,128)}, u32[]{:S(2)}) copy-start(f32[2,4,1440]{2,1,0:T(4,128)} %slope_hbm.1) | copy-start | bytes 138244
  4.3 0.8 %copy-start.4 = (f32[2,4,1440]{2,1,0:T(4,128)S(1)}, f32[2,4,1440]{2,1,0:T(4,128)}, u32[]{:S(2)}) copy-start(f32[2,4,1440]{2,1,0:T(4,128)} %wind_hbm.1) | copy-start | bytes 138244
  5.1 0.7 %copy-start.5 = (s32[4,1440]{1,0:T(4,128)S(1)}, s32[4,1440]{1,0:T(4,128)}, u32[]{:S(2)}) copy-start(s32[4,1440]{1,0:T(4,128)} %depth_hbm.1) | copy-start | bytes 69124
  5.8 0.7 %copy-start.6 = (s32[4,1440]{1,0:T(4,128)S(1)}, s32[4,1440]{1,0:T(4,128)}, u32[]{:S(2)}) copy-start(s32[4,1440]{1,0:T(4,128)} %land_hbm.1) | copy-start | bytes 69124
  6.6 0.7 %copy-start.7 = (f32[64,32]{0,1:T(8,128)S(1)}, f32[64,32]{0,1:T(8,128)}, u32[]{:S(2)}) copy-start(f32[64,32]{0,1:T(8,128)} %param.12) | copy-start | bytes 24580
  7.3 0.7 %copy-start.8 = (f32[8,128]{1,0:T(8,128)S(1)}, f32[8,128]{1,0:T(8,128)}, u32[]{:S(2)}) copy-start(f32[8,128]{1,0:T(8,128)} %constant.4.clone.scalars_hbm) | copy-start | bytes 12292

commit v5 on v4

--- a/solution.py
+++ b/solution.py
@@ -189,7 +189,7 @@
             hs_ref[1, j, rows, :] = jnp.concatenate(high, axis=0).astype(jnp.bfloat16)
         return carry
 
-    lax.fori_loop(0, ND // 4, prepare, 0)
+    lax.fori_loop(0, ND // 4, prepare, 0, unroll=3)
 
     pl.semaphore_wait(barrier, len(OFFSETS) + 2)
     halos = []
@@ -231,7 +231,7 @@
             adv_ref[j, pl.ds(base, 8), :] = out
         return carry
 
-    lax.fori_loop(0, ND, along, 0, unroll=2)
+    lax.fori_loop(0, ND, along, 0, unroll=4)
 
     keep_dn = (band < bands - 1).astype(jnp.float32)
     keep_up = (band > 0).astype(jnp.float32)
@@ -264,7 +264,7 @@
                     adv_ref[j, here, :] = (adv_ref[j, here, :] - flux) * fl_ref[F_SEA, j]
             return carry
 
-        lax.fori_loop(0, ND // 4, across, 0, unroll=1)
+        lax.fori_loop(0, ND // 4, across, 0, unroll=3)
 
         def refract(d, sums):
             cos_d = scalars_ref[0, d]
@@ -283,7 +283,7 @@
                 t_ref[j, pl.ds(d, 8, stride=ND), :] = out
             return tuple(sums)
 
-        sums = lax.fori_loop(0, ND, refract, (zero,) * PER, unroll=3)
+        sums = lax.fori_loop(0, ND, refract, (zero,) * PER, unroll=6)
         for i in range(PER):
             j = PER * c + i
             sq_ref[...] = sums[i] + pltpu.roll(sums[i], 7, 0)
@@ -359,7 +359,7 @@
                 grown_ref[3 * c + j, rows, :] = stage_ref[k, rows, :] * jnp.exp(jnp.maximum(push - calm[m], 0.0))
         return carry
 
-    lax.fori_loop(0, BLOCKS, grow, 0)
+    lax.fori_loop(0, BLOCKS, grow, 0, unroll=2)
     for copy in sums_z:
         copy.wait()
     for m in range(GROUPS // 8):
@@ -377,7 +377,7 @@
         dec_ref[k] = acc
         return acc
 
-    lax.fori_loop(0, STEPS, strengths, zero, unroll=16)
+    lax.fori_loop(0, STEPS, strengths, zero, unroll=32)
 
     fade0 = scalars_ref[4, FREQS * me]
     fade1 = scalars_ref[4, FREQS * me + 1]
@@ -602,7 +602,7 @@
             dma((BLOCKS - 1,)),
         ],
         compiler_params=pltpu.CompilerParams(
-            collective_id=0, has_side_effects=True, vmem_limit_bytes=40 * 1024 * 1024
+            collective_id=0, has_side_effects=True, vmem_limit_bytes=58 * 1024 * 1024
         ),
         name="wave_step",
     )(

time: 46.6 us -> 39.4 us (0.85)
  local copies, waits for them, and re-layouts: 7.98 us -> 1.13 us
    unnamed x20 -> x2, local copies, waits for them, and re-layouts: 7.98 us -> 1.13 us
where the time goes in v5:
time: 39.4 us; the launch traced here: 39.2 us
  Pallas kernels  38.1 us (97%)
  local copies, waits for them, and re-layouts  1.13 us (3%)
    pallas_call x1, Pallas kernels, body(): pl.pallas_call(step_kernel, out_shape=jax.ShapeDtypeStruct((BLOCKS, PACK,...  36.6 us
    pallas_call x1, Pallas kernels, body(): pl.pallas_call(finish_kernel, out_shape=jax.ShapeDtypeStruct((SLOTS, BLOC...  1.52 us
    unnamed x2, local copies, waits for them, and re-layouts  1.13 us

profile of v5, /device:TPU:1, one launch (start us, length us, event | category | flops | bytes accessed | tf_op | source)
XLA Modules:
  0.0 39.2 jit_solution(13211290761050439359)
XLA Ops:
  0.0 36.6 %wave_step.1.rb_ref = bf16[16,192,128]{2,1,0:T(8,128)(2,1)} custom-call(f32[8,128]{1,0:T(8,128)} %constant.4.clone.scalars_hbm, f32[2,72,128]{2,1,0:T(8,128)} %constant.5.clone.compass_hbm, s32[1,16]{1,0:T(1,128)} %counts_hbm.1, bf16[2,36,4,1440]{3,2,1,0:T(4,128)(2,1)} %spec_hbm.1, s32[4,1440]{1,0:T(4,128)} %depth_hbm.1, f32[32,64]{1,0:T(8,128)} %bitcast.2, ...), custom_call_target="tpu_custom_call" | custom-call | tf_op jit(solution)/shard_map/wave_step/pallas_call | solution.py:553
  36.6 0.0 copy-start
  36.6 1.1 %copy-done = bf16[16,192,128]{2,1,0:T(8,128)(2,1)S(1)} copy-done((bf16[16,192,128]{2,1,0:T(8,128)(2,1)S(1)}, bf16[16,192,128]{2,1,0:T(8,128)(2,1)}, u32[]{:S(2)}) %copy-start) | copy-done | bytes 786456
  37.7 1.5 %finish.1 = bf16[315,1152]{1,0:T(8,128)(2,1)} custom-call(bf16[16,192,128]{2,1,0:T(8,128)(2,1)S(1)} %copy-done), custom_call_target="tpu_custom_call" | custom-call | tf_op jit(solution)/shard_map/finish/pallas_call | solution.py:621
Async XLA Ops:
  36.6 1.1 %copy-start = (bf16[16,192,128]{2,1,0:T(8,128)(2,1)S(1)}, bf16[16,192,128]{2,1,0:T(8,128)(2,1)}, u32[]{:S(2)}) copy-start(bf16[16,192,128]{2,1,0:T(8,128)(2,1)} %wave_step.1.rb_ref) | copy-start | bytes 2359300

commit v6 on v5

--- a/solution.py
+++ b/solution.py
@@ -27,6 +27,7 @@
 PACK = 192
 CHUNKS = 4
 PER = TILES // CHUNKS
+RUN = 6
 SIDE = 4
 
 AT_SPOT, AT_KEEP, AT_DELTA, AT_LEN, AT_COUNT, AT_LAST = range(6)
@@ -60,8 +61,8 @@
     rb_ref,
     scalars_ref, compass_ref, counts_ref, spec_ref, depth_ref, speed_ref, current_ref, slope_ref, wind_ref, land_ref,
     gust_ref, gusts_ref,
-    gs_ref, raw_ref, cls_ref, flag_ref, tabv_ref, tab_ref, loc_ref, x_ref, adv_ref, t_ref, stage_ref, grown_ref, idx_ref, dec_ref, fl_ref, hs_ref, hr_ref, sq_ref, part_ref, total_ref, level_ref, yr_ref, zr_ref, sb_ref,
-    in_sem, tab_sem, halo_send, halo_recv, sum_send, sum_recv, send_sem, recv_sem,
+    gs_ref, raw_ref, cls_ref, flag_ref, tabv_ref, tab_ref, loc_ref, x_ref, adv_ref, t_ref, stage_ref, grown_ref, idx_ref, dec_ref, fl_ref, hs_ref, hr_ref, sq_ref, part_ref, total_ref, level_ref, yr_ref, zr_ref, sb_ref, own_ref,
+    in_sem, tab_sem, own_sem, halo_send, halo_recv, sum_send, sum_recv, send_sem, recv_sem,
 ):
     arrivals = [
         pltpu.make_async_copy(src, dst, in_sem.at[i])
@@ -140,12 +141,13 @@
         if j == TILES - 1:
             cls = jnp.where(lane < tail, cls, 0)
         cel = jnp.take_along_axis(gs_ref[...], cls, axis=1)
-        sixth = cel * (1.0 / 6.0)
-        fl_ref[F_SEA, j] = raw(0)
+        sea = raw(0)
+        sixth = cel * (sea * (1.0 / 6.0))
+        fl_ref[F_SEA, j] = sea
         fl_ref[F_CX, j] = sixth * stretch
         fl_ref[F_CY, j] = sixth
-        fl_ref[F_CUR0, j] = raw(1) * (1.0 / 6.0)
-        fl_ref[F_CUR1, j] = raw(2) * (1.0 / 6.0)
+        fl_ref[F_CUR0, j] = raw(1) * (sea * (1.0 / 6.0))
+        fl_ref[F_CUR1, j] = raw(2) * (sea * (1.0 / 6.0))
         fl_ref[F_T0, j] = (TURNING_SCALE * sixth) * raw(3)
         fl_ref[F_T1, j] = (TURNING_SCALE * sixth) * raw(4)
 
@@ -226,9 +228,7 @@
             far_ahead = jnp.where(lane >= LANES - 2, l2[after], l2[j])
             speed = fl_ref[F_CX, j] * cos_d + fl_ref[F_CUR0, j]
             out = x[j] - upwind12(far_behind, behind, x[j], ahead, far_ahead, speed)
-            if j == TILES - 1:
-                out = jnp.where(lane < tail, out, 0.0)
-            adv_ref[j, pl.ds(base, 8), :] = out
+            adv_ref[j, pl.ds(base + 16, 8), :] = out
         return carry
 
     lax.fori_loop(0, ND, along, 0, unroll=4)
@@ -236,6 +236,32 @@
     keep_dn = (band < bands - 1).astype(jnp.float32)
     keep_up = (band > 0).astype(jnp.float32)
     zero = jnp.zeros((8, LANES), jnp.float32)
+
+    def reduce_start(axis, c, src, dst):
+        copies = []
+        for i in range(1, SIDE):
+            o = (0, i) if axis == 0 else (i, 0)
+            copy = pltpu.make_async_remote_copy(
+                src_ref=src.at[c],
+                dst_ref=dst.at[c, i - 1],
+                send_sem=sum_send.at[axis, c, i - 1],
+                recv_sem=sum_recv.at[axis, c, i - 1],
+                device_id={"comp": peer(o)},
+                device_id_type=MESH,
+            )
+            copy.start()
+            copies.append(copy)
+        return copies
+
+    sums_y, sums_z = [], []
+
+    def pass_on(c):
+        for copy in sums_y[c]:
+            copy.wait()
+        total_ref[c] = (part_ref[c] + yr_ref[c, 0]) + (yr_ref[c, 1] + yr_ref[c, 2])
+        sums_z.append(reduce_start(1, c, total_ref, zr_ref))
+
+    part_ref[...] = jnp.zeros((CHUNKS, 16, LANES), jnp.float32)
 
     for c in range(CHUNKS):
         halos[2 * c].wait_recv()
@@ -261,49 +287,38 @@
                     behind = pltpu.roll(jnp.where(row == 3, h, v), 2, 0)
                     speed = fl_ref[F_CY, j] * scalars_ref[1, 4 * q + i] + fl_ref[F_CUR1, j]
                     flux = upwind12(far_behind, behind, v, ahead, far_ahead, speed)
-                    adv_ref[j, here, :] = (adv_ref[j, here, :] - flux) * fl_ref[F_SEA, j]
+                    there = pl.ds(base + (8 * i + 16), 8)
+                    adv_ref[j, there, :] = adv_ref[j, there, :] - flux
             return carry
 
         lax.fori_loop(0, ND // 4, across, 0, unroll=3)
 
-        def refract(d, sums):
-            cos_d = scalars_ref[0, d]
-            sin_d = scalars_ref[1, d]
-
-            def at(shift):
-                return pl.multiple_of(8 * lax.rem(d + (shift + ND), ND), 8)
-
-            places = [at(s) for s in (-2, -1, 0, 1, 2)]
+        for j in range(PER * c, PER * c + PER):
+            adv_ref[j, pl.ds(0, 16), :] = adv_ref[j, pl.ds(8 * ND, 16), :]
+            adv_ref[j, pl.ds(8 * ND + 16, 16), :] = adv_ref[j, pl.ds(16, 16), :]
+
+        def refract(q, sums):
+            base = pl.multiple_of(8 * RUN * q, 8)
             sums = list(sums)
             for j in range(PER * c, PER * c + PER):
-                values = [adv_ref[j, pl.ds(p, 8), :] for p in places]
-                speed = fl_ref[F_T0, j] * sin_d - fl_ref[F_T1, j] * cos_d
-                out = (values[2] - upwind12(*values, speed)) * fl_ref[F_SEA, j]
-                sums[j - PER * c] = sums[j - PER * c] + out * out
-                t_ref[j, pl.ds(d, 8, stride=ND), :] = out
+                near = [adv_ref[j, pl.ds(base + 8 * i, 8), :] for i in range(RUN + 4)]
+                t0, t1 = fl_ref[F_T0, j], fl_ref[F_T1, j]
+                for i in range(RUN):
+                    d = RUN * q + i
+                    speed = t0 * scalars_ref[1, d] - t1 * scalars_ref[0, d]
+                    out = near[i + 2] - upwind12(*near[i : i + 5], speed)
+                    sums[j - PER * c] = sums[j - PER * c] + out * out
+                    t_ref[j, pl.ds(d, 8, stride=ND), :] = out
             return tuple(sums)
 
-        sums = lax.fori_loop(0, ND, refract, (zero,) * PER, unroll=6)
+        sums = lax.fori_loop(0, ND // RUN, refract, (zero,) * PER, unroll=2)
         for i in range(PER):
             j = PER * c + i
             sq_ref[...] = sums[i] + pltpu.roll(sums[i], 7, 0)
-            part_ref[pl.ds(4 * j, 4), :] = sq_ref[pl.ds(0, 4, stride=2), :]
-
-    def reduce_start(axis, src, dst):
-        copies = []
-        for i in range(1, SIDE):
-            o = (0, i) if axis == 0 else (i, 0)
-            copy = pltpu.make_async_remote_copy(
-                src_ref=src,
-                dst_ref=dst.at[i - 1],
-                send_sem=sum_send.at[axis, i - 1],
-                recv_sem=sum_recv.at[axis, i - 1],
-                device_id={"comp": peer(o)},
-                device_id_type=MESH,
-            )
-            copy.start()
-            copies.append(copy)
-        return copies
+            part_ref[c, pl.ds(4 * i, 4), :] = sq_ref[pl.ds(0, 4, stride=2), :]
+        sums_y.append(reduce_start(0, c, part_ref, yr_ref))
+        if c >= 2:
+            pass_on(c - 2)
 
     t_rows = t_ref.reshape(GROUPS, COMPS, LANES)
 
@@ -326,15 +341,11 @@
         gusts_ref[k] = gust
         return tuple(parts) + (gust,)
 
-    sums_y = reduce_start(0, part_ref, yr_ref)
     table_copy.wait()
-    lax.fori_loop(0, STEPS, step, (zero,) * (COMPS // 8 + 1), unroll=8)
-    for copy in sums_y:
-        copy.wait()
-    for m in range(GROUPS // 8):
-        rows = pl.ds(8 * m, 8)
-        total_ref[rows, :] = (part_ref[rows, :] + yr_ref[0, rows, :]) + (yr_ref[1, rows, :] + yr_ref[2, rows, :])
-    sums_z = reduce_start(1, total_ref, zr_ref)
+    carry = lax.fori_loop(0, STEPS // 2, step, (zero,) * (COMPS // 8 + 1), unroll=8)
+    pass_on(CHUNKS - 2)
+    pass_on(CHUNKS - 1)
+    lax.fori_loop(STEPS // 2, STEPS, step, carry, unroll=8)
 
     def by_row(q):
         low, high = scalars_ref[q, FREQS * me], scalars_ref[q, FREQS * me + 1]
@@ -360,14 +371,13 @@
         return carry
 
     lax.fori_loop(0, BLOCKS, grow, 0, unroll=2)
-    for copy in sums_z:
-        copy.wait()
-    for m in range(GROUPS // 8):
-        rows = pl.ds(8 * m, 8)
-        total = (total_ref[rows, :] + zr_ref[0, rows, :]) + (zr_ref[1, rows, :] + zr_ref[2, rows, :])
+    for c in range(CHUNKS):
+        for copy in sums_z[c]:
+            copy.wait()
+        total = (total_ref[c] + zr_ref[c, 0]) + (zr_ref[c, 1] + zr_ref[c, 2])
         total = jnp.sqrt(total * (1.0 / (BLOCKS * COMPS)) + 1e-6)
-        for i in range(8):
-            level_ref[8 * m + i] = jnp.broadcast_to(total[i : i + 1], (8, LANES))
+        for i in range(ROWS * PER):
+            level_ref[ROWS * PER * c + i] = jnp.broadcast_to(total[i : i + 1], (8, LANES))
 
     def strengths(k, acc):
         keep = tab_ref[AT_KEEP, k].astype(jnp.float32)
@@ -426,19 +436,26 @@
         copies.append(copy)
 
     def put_own(m, v):
-        rb_ref[me, pl.ds(16 * m, 16), :] = v
+        own_ref[pl.ds(16 * m, 16), :] = v
 
     block(me, put_own)
+    own_copy = pltpu.make_async_copy(own_ref, rb_ref.at[me], own_sem)
+    own_copy.start()
+    own_copy.wait()
     for copy in halos:
         copy.wait_send()
     for copy in copies:
         copy.wait()
 
 
-def finish_kernel(rb_ref, out_ref, v_ref):
+def finish_kernel(rb_ref, out_ref, in_ref, v_ref, in_sem):
+    copy = pltpu.make_async_copy(rb_ref, in_ref, in_sem)
+    copy.start()
+    copy.wait()
+
     def spread(i, carry):
         base = pl.multiple_of(COMPS * i, 8)
-        v = rb_ref[i].astype(jnp.float32)
+        v = in_ref[i].astype(jnp.float32)
         for j in range(2):
             v_ref[j, pl.ds(base, COMPS), :] = v[COMPS * j : COMPS * (j + 1)]
         v_ref[2, pl.ds(base, 40), :] = v[2 * COMPS : 2 * COMPS + 40]
@@ -554,7 +571,7 @@
         step_kernel,
         out_shape=jax.ShapeDtypeStruct((BLOCKS, PACK, LANES), bf16),
         in_specs=[pl.BlockSpec(memory_space=pltpu.HBM)] * 10,
-        out_specs=vmem,
+        out_specs=pl.BlockSpec(memory_space=pltpu.HBM),
         scratch_shapes=[
             pltpu.SMEM((8, LANES), f32),
             pltpu.VMEM((2, COMPS, LANES), f32),
@@ -576,7 +593,7 @@
             pltpu.SMEM((8, LANES), jnp.int32),
             pltpu.VMEM((GROUPS, 8, LANES), jnp.int32),
             pltpu.VMEM((TILES, 8 * ND, LANES), f32),
-            pltpu.VMEM((TILES, 8 * ND, LANES), f32),
+            pltpu.VMEM((TILES, 8 * (ND + 4), LANES), f32),
             pltpu.VMEM((TILES, 8 * ND, LANES), f32),
             pltpu.VMEM((STEPS, COMPS, LANES), f32),
             pltpu.VMEM((3 * BLOCKS, COMPS, LANES), f32),
@@ -586,18 +603,20 @@
             pltpu.VMEM((2, TILES, 4 * ND, LANES), bf16),
             pltpu.VMEM((2, TILES, 4 * ND, LANES), bf16),
             pltpu.VMEM((8, LANES), f32),
-            pltpu.VMEM((GROUPS, LANES), f32),
-            pltpu.VMEM((GROUPS, LANES), f32),
+            pltpu.VMEM((CHUNKS, 16, LANES), f32),
+            pltpu.VMEM((CHUNKS, 16, LANES), f32),
             pltpu.VMEM((GROUPS, 8, LANES), f32),
-            pltpu.VMEM((SIDE - 1, GROUPS, LANES), f32),
-            pltpu.VMEM((SIDE - 1, GROUPS, LANES), f32),
+            pltpu.VMEM((CHUNKS, SIDE - 1, 16, LANES), f32),
+            pltpu.VMEM((CHUNKS, SIDE - 1, 16, LANES), f32),
             pltpu.VMEM((BLOCKS - 1, PACK, LANES), bf16),
+            pltpu.VMEM((PACK, LANES), bf16),
             dma((10,)),
+            dma,
             dma,
             dma((2, CHUNKS)),
             dma((2, CHUNKS)),
-            dma((2, SIDE - 1)),
-            dma((2, SIDE - 1)),
+            dma((2, CHUNKS, SIDE - 1)),
+            dma((2, CHUNKS, SIDE - 1)),
             dma((BLOCKS - 1,)),
             dma((BLOCKS - 1,)),
         ],
@@ -621,10 +640,14 @@
     out = pl.pallas_call(
         finish_kernel,
         out_shape=jax.ShapeDtypeStruct((SLOTS, BLOCKS * COMPS), bf16),
-        in_specs=[vmem],
+        in_specs=[pl.BlockSpec(memory_space=pltpu.HBM)],
         out_specs=vmem,
-        scratch_shapes=[pltpu.VMEM((3, BLOCKS * COMPS, LANES), f32)],
-        compiler_params=pltpu.CompilerParams(vmem_limit_bytes=16 * 1024 * 1024),
+        scratch_shapes=[
+            pltpu.VMEM((BLOCKS, PACK, LANES), bf16),
+            pltpu.VMEM((3, BLOCKS * COMPS, LANES), f32),
+            dma,
+        ],
+        compiler_params=pltpu.CompilerParams(vmem_limit_bytes=58 * 1024 * 1024),
         name="finish",
     )(rb)
     return out.T

time: 39.4 us -> 37.6 us (0.954)
  local copies, waits for them, and re-layouts: 1.13 us -> 0 us
  Pallas kernels: 38.1 us -> 37.4 us
    pallas_call x1, Pallas kernels: 36.6 us -> 34.7 us  [body(): pl.pallas_call(step_kernel, out_shape=jax.ShapeDtypeStruct((BLOCKS, PACK,...]
    pallas_call x1, Pallas kernels: 1.52 us -> 2.67 us  [body(): pl.pallas_call(finish_kernel, out_shape=jax.ShapeDtypeStruct((SLOTS, BLOC...]
    unnamed x2 -> x0, local copies, waits for them, and re-layouts: 1.13 us -> none
where the time goes in v6:
time: 37.6 us; the launch traced here: 37.4 us
  Pallas kernels  37.4 us (99%)
    pallas_call x1, Pallas kernels, body(): pl.pallas_call(step_kernel, out_shape=jax.ShapeDtypeStruct((BLOCKS, PACK,...  34.7 us
    pallas_call x1, Pallas kernels, body(): pl.pallas_call(finish_kernel, out_shape=jax.ShapeDtypeStruct((SLOTS, BLOC...  2.67 us

profile of v6, /device:TPU:1, one launch (start us, length us, event | category | flops | bytes accessed | tf_op | source)
XLA Modules:
  0.0 37.4 jit_solution(15314969472247944739)
XLA Ops:
  0.0 34.7 %wave_step.1.rb_ref = bf16[16,192,128]{2,1,0:T(8,128)(2,1)} custom-call(f32[8,128]{1,0:T(8,128)} %constant.4.clone.scalars_hbm, f32[2,72,128]{2,1,0:T(8,128)} %constant.5.clone.compass_hbm, s32[1,16]{1,0:T(1,128)} %counts_hbm.1, bf16[2,36,4,1440]{3,2,1,0:T(4,128)(2,1)} %spec_hbm.1, s32[4,1440]{1,0:T(4,128)} %depth_hbm.1, f32[32,64]{1,0:T(8,128)} %bitcast.2, ...), custom_call_target="tpu_custom_call" | custom-call | tf_op jit(solution)/shard_map/wave_step/pallas_call | solution.py:570
  34.7 2.7 %finish.1 = bf16[315,1152]{1,0:T(8,128)(2,1)} custom-call(bf16[16,192,128]{2,1,0:T(8,128)(2,1)} %wave_step.1.rb_ref), custom_call_target="tpu_custom_call" | custom-call | tf_op jit(solution)/shard_map/finish/pallas_call | solution.py:640

commit v7 on v6

--- a/solution.py
+++ b/solution.py
@@ -25,7 +25,7 @@
 STEPS = 96
 COMPS = FREQS * ND
 PACK = 192
-CHUNKS = 4
+CHUNKS = 3
 PER = TILES // CHUNKS
 RUN = 6
 SIDE = 4
@@ -195,7 +195,8 @@
 
     pl.semaphore_wait(barrier, len(OFFSETS) + 2)
     halos = []
-    for c in range(CHUNKS):
+
+    def send_halos(c):
         for side, b in ((0, south), (1, north)):
             copy = pltpu.make_async_remote_copy(
                 src_ref=hs_ref.at[side, pl.ds(PER * c, PER)],
@@ -208,9 +209,15 @@
             copy.start()
             halos.append(copy)
 
+    for c in range(CHUNKS // 2):
+        send_halos(c)
+
     build_tables(counts_ref, flag_ref, tabv_ref, loc_ref)
     table_copy = pltpu.make_async_copy(tabv_ref, tab_ref, tab_sem)
     table_copy.start()
+
+    for c in range(CHUNKS // 2, CHUNKS):
+        send_halos(c)
 
     def along(d, carry):
         base = pl.multiple_of(8 * d, 8)
@@ -291,7 +298,7 @@
                     adv_ref[j, there, :] = adv_ref[j, there, :] - flux
             return carry
 
-        lax.fori_loop(0, ND // 4, across, 0, unroll=3)
+        lax.fori_loop(0, ND // 4, across, 0)
 
         for j in range(PER * c, PER * c + PER):
             adv_ref[j, pl.ds(0, 16), :] = adv_ref[j, pl.ds(8 * ND, 16), :]
@@ -311,7 +318,7 @@
                     t_ref[j, pl.ds(d, 8, stride=ND), :] = out
             return tuple(sums)
 
-        sums = lax.fori_loop(0, ND // RUN, refract, (zero,) * PER, unroll=2)
+        sums = lax.fori_loop(0, ND // RUN, refract, (zero,) * PER)
         for i in range(PER):
             j = PER * c + i
             sq_ref[...] = sums[i] + pltpu.roll(sums[i], 7, 0)
@@ -449,9 +456,11 @@
 
 
 def finish_kernel(rb_ref, out_ref, in_ref, v_ref, in_sem):
-    copy = pltpu.make_async_copy(rb_ref, in_ref, in_sem)
-    copy.start()
-    copy.wait()
+    copies = [
+        pltpu.make_async_copy(rb_ref.at[pl.ds(4 * i, 4)], in_ref.at[pl.ds(4 * i, 4)], in_sem.at[i]) for i in range(4)
+    ]
+    for copy in copies:
+        copy.start()
 
     def spread(i, carry):
         base = pl.multiple_of(COMPS * i, 8)
@@ -462,7 +471,9 @@
         v_ref[2, pl.ds(base + 40, 32), :] = pltpu.roll(v[2 * COMPS : 2 * COMPS + 32], 64, 1)
         return carry
 
-    lax.fori_loop(0, BLOCKS, spread, 0, unroll=4)
+    for i in range(4):
+        copies[i].wait()
+        lax.fori_loop(4 * i, 4 * i + 4, spread, 0, unroll=4)
     for m in range(BLOCKS * COMPS // LANES):
         for j in range(3):
             block = v_ref[j, pl.ds(LANES * m, LANES), :].T.astype(jnp.bfloat16)
@@ -645,7 +656,7 @@
         scratch_shapes=[
             pltpu.VMEM((BLOCKS, PACK, LANES), bf16),
             pltpu.VMEM((3, BLOCKS * COMPS, LANES), f32),
-            dma,
+            dma((4,)),
         ],
         compiler_params=pltpu.CompilerParams(vmem_limit_bytes=58 * 1024 * 1024),
         name="finish",

time: 37.6 us -> 36.6 us (0.973)
  Pallas kernels: 37.4 us -> 36.3 us
    pallas_call x1, Pallas kernels: 34.7 us -> 33.8 us  [body(): pl.pallas_call(step_kernel, out_shape=jax.ShapeDtypeStruct((BLOCKS, PACK,...]
where the time goes in v7:
time: 36.6 us; the launch traced here: 36.3 us
  Pallas kernels  36.3 us (99%)
    pallas_call x1, Pallas kernels, body(): pl.pallas_call(step_kernel, out_shape=jax.ShapeDtypeStruct((BLOCKS, PACK,...  33.8 us
    pallas_call x1, Pallas kernels, body(): pl.pallas_call(finish_kernel, out_shape=jax.ShapeDtypeStruct((SLOTS, BLOC...  2.44 us

profile of v7, /device:TPU:1, one launch (start us, length us, event | category | flops | bytes accessed | tf_op | source)
XLA Modules:
  0.0 36.3 jit_solution(13177980876838951775)
XLA Ops:
  0.0 33.8 %wave_step.1.rb_ref = bf16[16,192,128]{2,1,0:T(8,128)(2,1)} custom-call(f32[8,128]{1,0:T(8,128)} %constant.4.clone.scalars_hbm, f32[2,72,128]{2,1,0:T(8,128)} %constant.5.clone.compass_hbm, s32[1,16]{1,0:T(1,128)} %counts_hbm.1, bf16[2,36,4,1440]{3,2,1,0:T(4,128)(2,1)} %spec_hbm.1, s32[4,1440]{1,0:T(4,128)} %depth_hbm.1, f32[32,64]{1,0:T(8,128)} %bitcast.2, ...), custom_call_target="tpu_custom_call" | custom-call | tf_op jit(solution)/shard_map/wave_step/pallas_call | solution.py:581
  33.8 2.4 %finish.1 = bf16[315,1152]{1,0:T(8,128)(2,1)} custom-call(bf16[16,192,128]{2,1,0:T(8,128)(2,1)} %wave_step.1.rb_ref), custom_call_target="tpu_custom_call" | custom-call | tf_op jit(solution)/shard_map/finish/pallas_call | solution.py:651

commit v8 on v7

--- a/solution.py
+++ b/solution.py
@@ -1,3 +1,4 @@
+import functools
 import math
 
 import jax
@@ -162,17 +163,15 @@
 
     lax.fori_loop(0, ND, load, 0)
 
-    def prepare(q, carry):
+    def prepare(c, q, carry):
         base = pl.multiple_of(32 * q, 32)
-        first = [None] * 4
-        for j in range(TILES):
+        for j in range(PER * c, PER * c + PER):
             v = [x_ref[j, pl.ds(base + 8 * i, 8), :] for i in range(4)]
             if j == TILES - 1:
                 v = [jnp.where(lane < tail, w, 0.0) for w in v]
             v = [w * fl_ref[F_SEA, j] for w in v]
-            if j == 0:
-                first = v
             if j == TILES - 1:
+                first = [x_ref[0, pl.ds(base + 8 * i, 8), :] for i in range(4)]
                 v = [
                     jnp.where(
                         lane < tail,
@@ -191,9 +190,6 @@
             hs_ref[1, j, rows, :] = jnp.concatenate(high, axis=0).astype(jnp.bfloat16)
         return carry
 
-    lax.fori_loop(0, ND // 4, prepare, 0, unroll=3)
-
-    pl.semaphore_wait(barrier, len(OFFSETS) + 2)
     halos = []
 
     def send_halos(c):
@@ -209,15 +205,15 @@
             copy.start()
             halos.append(copy)
 
-    for c in range(CHUNKS // 2):
+    for c in range(CHUNKS):
+        lax.fori_loop(0, ND // 4, functools.partial(prepare, c), 0, unroll=3)
+        if c == 0:
+            pl.semaphore_wait(barrier, len(OFFSETS) + 2)
         send_halos(c)
 
     build_tables(counts_ref, flag_ref, tabv_ref, loc_ref)
     table_copy = pltpu.make_async_copy(tabv_ref, tab_ref, tab_sem)
     table_copy.start()
-
-    for c in range(CHUNKS // 2, CHUNKS):
-        send_halos(c)
 
     def along(d, carry):
         base = pl.multiple_of(8 * d, 8)

time: 36.6 us -> 36.5 us (level)
  no operation moved by 1% of the time
where the time goes in v8:
time: 36.5 us; the launch traced here: 36.2 us
  Pallas kernels  36.2 us (99%)
    pallas_call x1, Pallas kernels, body(): pl.pallas_call(step_kernel, out_shape=jax.ShapeDtypeStruct((BLOCKS, PACK,...  33.8 us
    pallas_call x1, Pallas kernels, body(): pl.pallas_call(finish_kernel, out_shape=jax.ShapeDtypeStruct((SLOTS, BLOC...  2.44 us

profile of v8, /device:TPU:1, one launch (start us, length us, event | category | flops | bytes accessed | tf_op | source)
XLA Modules:
  0.0 36.2 jit_solution(1707384127138887718)
XLA Ops:
  0.0 33.8 %wave_step.1.rb_ref = bf16[16,192,128]{2,1,0:T(8,128)(2,1)} custom-call(f32[8,128]{1,0:T(8,128)} %constant.4.clone.scalars_hbm, f32[2,72,128]{2,1,0:T(8,128)} %constant.5.clone.compass_hbm, s32[1,16]{1,0:T(1,128)} %counts_hbm.1, bf16[2,36,4,1440]{3,2,1,0:T(4,128)(2,1)} %spec_hbm.1, s32[4,1440]{1,0:T(4,128)} %depth_hbm.1, f32[32,64]{1,0:T(8,128)} %bitcast.2, ...), custom_call_target="tpu_custom_call" | custom-call | tf_op jit(solution)/shard_map/wave_step/pallas_call | solution.py:577
  33.8 2.4 %finish.1 = bf16[315,1152]{1,0:T(8,128)(2,1)} custom-call(bf16[16,192,128]{2,1,0:T(8,128)(2,1)} %wave_step.1.rb_ref), custom_call_target="tpu_custom_call" | custom-call | tf_op jit(solution)/shard_map/finish/pallas_call | solution.py:647

commit v9 on v7

--- a/solution.py
+++ b/solution.py
@@ -387,10 +387,9 @@
             level_ref[ROWS * PER * c + i] = jnp.broadcast_to(total[i : i + 1], (8, LANES))
 
     def strengths(k, acc):
-        keep = tab_ref[AT_KEEP, k].astype(jnp.float32)
         idx = idx_ref[k]
         got = jnp.take_along_axis(level_ref[tab_ref[AT_SPOT, k]], jnp.maximum(idx, 0), axis=1)
-        acc = jnp.where(idx >= 0, got, acc * keep)
+        acc = jnp.where(idx >= 0, got, acc)
         dec_ref[k] = acc
         return acc
 
@@ -474,11 +473,15 @@
     for i in range(4):
         copies[i].wait()
         lax.fori_loop(4 * i, 4 * i + 4, spread, 0, unroll=4)
-    for m in range(BLOCKS * COMPS // LANES):
+    def turn(m, carry):
+        at = pl.multiple_of(LANES * m, LANES)
         for j in range(3):
-            block = v_ref[j, pl.ds(LANES * m, LANES), :].T.astype(jnp.bfloat16)
+            block = v_ref[j, pl.ds(at, LANES), :].T.astype(jnp.bfloat16)
             rows = min(LANES, SLOTS - LANES * j)
-            out_ref[pl.ds(LANES * j, rows), pl.ds(LANES * m, LANES)] = block[:rows]
+            out_ref[pl.ds(LANES * j, rows), pl.ds(at, LANES)] = block[:rows]
+        return carry
+
+    lax.fori_loop(0, BLOCKS * COMPS // LANES, turn, 0)
 
 
 def build_tables(counts_ref, flag_ref, tabv_ref, loc_ref):

time: 36.6 us -> 37.3 us (1.019)
  Pallas kernels: 36.3 us -> 36.9 us
    pallas_call x1, Pallas kernels: 2.44 us -> 3.14 us  [body(): pl.pallas_call(finish_kernel, out_shape=jax.ShapeDtypeStruct((SLOTS, BLOC...]
where the time goes in v9:
time: 37.3 us; the launch traced here: 37 us
  Pallas kernels  36.9 us (99%)
    pallas_call x1, Pallas kernels, body(): pl.pallas_call(step_kernel, out_shape=jax.ShapeDtypeStruct((BLOCKS, PACK,...  33.8 us
    pallas_call x1, Pallas kernels, body(): pl.pallas_call(finish_kernel, out_shape=jax.ShapeDtypeStruct((SLOTS, BLOC...  3.14 us

profile of v9, /device:TPU:1, one launch (start us, length us, event | category | flops | bytes accessed | tf_op | source)
XLA Modules:
  0.0 37.0 jit_solution(18418978703860320394)
XLA Ops:
  0.0 33.8 %wave_step.1.rb_ref = bf16[16,192,128]{2,1,0:T(8,128)(2,1)} custom-call(f32[8,128]{1,0:T(8,128)} %constant.4.clone.scalars_hbm, f32[2,72,128]{2,1,0:T(8,128)} %constant.5.clone.compass_hbm, s32[1,16]{1,0:T(1,128)} %counts_hbm.1, bf16[2,36,4,1440]{3,2,1,0:T(4,128)(2,1)} %spec_hbm.1, s32[4,1440]{1,0:T(4,128)} %depth_hbm.1, f32[32,64]{1,0:T(8,128)} %bitcast.2, ...), custom_call_target="tpu_custom_call" | custom-call | tf_op jit(solution)/shard_map/wave_step/pallas_call | solution.py:584
  33.8 3.1 %finish.1 = bf16[315,1152]{1,0:T(8,128)(2,1)} custom-call(bf16[16,192,128]{2,1,0:T(8,128)(2,1)} %wave_step.1.rb_ref), custom_call_target="tpu_custom_call" | custom-call | tf_op jit(solution)/shard_map/finish/pallas_call | solution.py:654

commit v10 on v7

--- a/solution.py
+++ b/solution.py
@@ -387,10 +387,9 @@
             level_ref[ROWS * PER * c + i] = jnp.broadcast_to(total[i : i + 1], (8, LANES))
 
     def strengths(k, acc):
-        keep = tab_ref[AT_KEEP, k].astype(jnp.float32)
         idx = idx_ref[k]
         got = jnp.take_along_axis(level_ref[tab_ref[AT_SPOT, k]], jnp.maximum(idx, 0), axis=1)
-        acc = jnp.where(idx >= 0, got, acc * keep)
+        acc = jnp.where(idx >= 0, got, acc)
         dec_ref[k] = acc
         return acc
 

time: 36.6 us -> 36.6 us (level)
  no operation moved by 1% of the time
where the time goes in v10:
time: 36.6 us; the launch traced here: 36.3 us
  Pallas kernels  36.2 us (99%)
    pallas_call x1, Pallas kernels, body(): pl.pallas_call(step_kernel, out_shape=jax.ShapeDtypeStruct((BLOCKS, PACK,...  33.8 us
    pallas_call x1, Pallas kernels, body(): pl.pallas_call(finish_kernel, out_shape=jax.ShapeDtypeStruct((SLOTS, BLOC...  2.44 us

profile of v10, /device:TPU:1, one launch (start us, length us, event | category | flops | bytes accessed | tf_op | source)
XLA Modules:
  0.0 36.3 jit_solution(5357494126224297771)
XLA Ops:
  0.0 33.8 %wave_step.1.rb_ref = bf16[16,192,128]{2,1,0:T(8,128)(2,1)} custom-call(f32[8,128]{1,0:T(8,128)} %constant.4.clone.scalars_hbm, f32[2,72,128]{2,1,0:T(8,128)} %constant.5.clone.compass_hbm, s32[1,16]{1,0:T(1,128)} %counts_hbm.1, bf16[2,36,4,1440]{3,2,1,0:T(4,128)(2,1)} %spec_hbm.1, s32[4,1440]{1,0:T(4,128)} %depth_hbm.1, f32[32,64]{1,0:T(8,128)} %bitcast.2, ...), custom_call_target="tpu_custom_call" | custom-call | tf_op jit(solution)/shard_map/wave_step/pallas_call | solution.py:580
  33.8 2.4 %finish.1 = bf16[315,1152]{1,0:T(8,128)(2,1)} custom-call(bf16[16,192,128]{2,1,0:T(8,128)(2,1)} %wave_step.1.rb_ref), custom_call_target="tpu_custom_call" | custom-call | tf_op jit(solution)/shard_map/finish/pallas_call | solution.py:650
